TPU v7x, 512 devices: a whole 4x8x8 slice. The times are simulated.
512 devices in a mesh: ctx: 64 (over x, z, core), tp: 8 (over y).
Axes of the slice: x: 4, y: 8, z: 8, core: 2. Of those that a mesh axis runs over, the one named last changes fastest.
Arguments:
- tokens: bfloat16 [32768, 2048], P('ctx', 'tp'), may hold values from -2 to 2
- w_query: bfloat16 [2048, 2048], P('ctx', 'tp'), may hold values from -0.125 to 0.125
- w_key: bfloat16 [2048, 2048], P('ctx', 'tp'), may hold values from -0.125 to 0.125
- w_value: bfloat16 [2048, 2048], P('ctx', 'tp'), may hold values from -0.125 to 0.125
- features: float32 [16, 256, 128], P('tp'), may hold values from -4 to 4
- w_out: bfloat16 [2048, 2048], P('tp', 'ctx'), may hold values from -0.125 to 0.125
Outputs:
- mixed: bfloat16 [32768, 2048], P('ctx', 'tp')
All inputs are finite; a program needn't handle non-finite values.
Results may differ from a plain program's by a relative error of at most 0.022.
Values may be sent and summed in bfloat16 or wider, within the bound.
A program may use at most 64 MiB of HBM per device.

v0:
```python
import jax
import jax.numpy as jnp
from jax import lax
from jax.sharding import PartitionSpec as P

TOP_PRECISION = lax.Precision.HIGHEST


def carried_in(shard, axis, join, neutral):
    place = lax.axis_index(axis)
    gathered = jax.tree.map(
        lambda a, kind: lax.all_gather(a.astype(kind), axis), shard, (jnp.bfloat16, jnp.bfloat16)
    )
    state = jax.tree.map(lambda a, e: jnp.zeros_like(a) + jnp.asarray(e, a.dtype), shard, neutral)

    def one(hop, state):
        return join(
            state,
            jax.tree.map(
                lambda a, own: lax.dynamic_index_in_dim(a, hop, 0, False).astype(own.dtype),
                gathered,
                shard,
            ),
        )

    return lax.fori_loop(0, place, one, state)


def positive(projected, features):
    count = projected.shape[0]
    heads = features.shape[0]
    width = features.shape[2]
    scaled_logits = projected.reshape(count, heads, width) * width ** (-0.25)
    feature_logits = jnp.einsum("rxy,xzy->xrz", scaled_logits, features, precision=TOP_PRECISION)
    half_square = 0.5 * jnp.sum(scaled_logits * scaled_logits, axis=-1)
    return jnp.exp(feature_logits - jnp.transpose(half_square)[:, :, None])


def combine_sums(earlier, later):
    return (earlier[0] + later[0], earlier[1] + later[1])


def body(tokens, w_query, w_key, w_value, features, w_out):
    whole = lax.all_gather(tokens, "tp", axis=1, tiled=True)
    count = whole.shape[0]
    full_query, full_key, full_value = (
        lax.all_gather(w_query, "ctx", axis=0, tiled=True),
        lax.all_gather(w_key, "ctx", axis=0, tiled=True),
        lax.all_gather(w_value, "ctx", axis=0, tiled=True),
    )
    query = jnp.dot(whole, full_query, preferred_element_type=jnp.float32)
    key = jnp.dot(whole, full_key, preferred_element_type=jnp.float32)
    value = jnp.dot(whole, full_value, preferred_element_type=jnp.float32)
    heads = features.shape[0]
    feats = features.shape[1]
    width = features.shape[2]
    block = min(count, 512)
    blocks = count // block
    query_feature_map = positive(query, features).reshape(heads, blocks, block, feats)
    key_feature_map = positive(key, features).reshape(heads, blocks, block, feats)
    per_head_value = jnp.transpose(value.reshape(count, heads, width), (1, 0, 2)).reshape(
        heads, blocks, block, width
    )
    block_state = jnp.einsum(
        "hnkm,hnkd->hnmd", key_feature_map, per_head_value, precision=TOP_PRECISION
    )
    block_normal = jnp.sum(key_feature_map, axis=2)
    local_state = jnp.sum(block_state, axis=1)
    local_normal = jnp.sum(block_normal, axis=1)
    earlier_state = jnp.concatenate(
        [jnp.zeros_like(block_state), jnp.cumsum(block_state, axis=1)[:, :-1]], axis=1
    )
    earlier_normal = jnp.concatenate(
        [jnp.zeros_like(block_normal), jnp.cumsum(block_normal, axis=1)[:, :-1]], axis=1
    )
    causal = jnp.tril(jnp.ones((block, block), dtype=bool))
    prefix_state, prefix_normal = carried_in(
        (local_state, local_normal),
        "ctx",
        combine_sums,
        (jnp.zeros_like(local_state), jnp.zeros_like(local_normal)),
    )
    scores = jnp.einsum(
        "hnqm,hnkm->hnqk", query_feature_map, key_feature_map, precision=TOP_PRECISION
    )
    scores = jnp.where(causal, scores, jnp.float32(0.0))
    numer_in = jnp.einsum("hnqk,hnkd->hnqd", scores, per_head_value, precision=TOP_PRECISION)
    numerator_sum = numer_in
    denom = jnp.sum(scores, axis=-1)
    numer_cross = jnp.einsum(
        "hnqm,hnmd->hnqd",
        query_feature_map,
        earlier_state + prefix_state[:, None],
        precision=TOP_PRECISION,
    )
    denom_cross = jnp.einsum(
        "hnqm,hnm->hnq",
        query_feature_map,
        earlier_normal + prefix_normal[:, None],
        precision=TOP_PRECISION,
    )
    numer_cross, denom_cross = (numer_cross, denom_cross)
    numerator_sum = numerator_sum + numer_cross
    denom = denom + denom_cross
    attn = (numerator_sum / denom[..., None]).astype(jnp.bfloat16)
    attn = jnp.transpose(attn.reshape(heads, count, width), (1, 0, 2)).reshape(count, heads * width)
    terms = jnp.dot(
        attn, lax.all_gather(w_out, "ctx", axis=1, tiled=True), preferred_element_type=jnp.float32
    )
    return lax.psum_scatter(terms.astype(jnp.bfloat16), "tp", scatter_dimension=1, tiled=True)


def solution(mesh):
    return jax.shard_map(
        body,
        mesh=mesh,
        in_specs=(
            P("ctx", "tp"),
            P("ctx", "tp"),
            P("ctx", "tp"),
            P("ctx", "tp"),
            P("tp", None, None),
            P("tp", "ctx"),
        ),
        out_specs=P("ctx", "tp"),
        check_vma=False,
    )
```

profile of v0, /device:TPU:1, one launch (start us, length us, event | category | flops | bytes accessed | tf_op | source)
XLA Modules:
  0.0 536.4 jit_solution(3460628607526896380)
XLA Ops:
  6.5 0.7 all-gather.16.cloned.1.call-update
  7.3 0.7 all-gather.10.cloned.1.call-update
  8.1 0.7 all-gather.14.cloned.1.call-update
  9.4 89.8 %all-gather.16.cloned.1.call-done = bf16[2048,256]{1,0:T(8,128)(2,1)} async-done(((bf16[32,256]{1,0:T(8,128)(2,1)}), bf16[2048,256]{1,0:T(8,128)(2,1)}) %all-gather.16.cloned.1.call-update) | async-done | bytes 1048592 | tf_op jit(solution)/shard_map/all_gather | solution.py:49
  99.2 44.8 %all-gather.10.cloned.1.call-done = bf16[512,2048]{1,0:T(8,128)(2,1)} async-done(((bf16[512,256]{1,0:T(8,128)(2,1)}), bf16[512,2048]{1,0:T(8,128)(2,1)}) %all-gather.10.cloned.1.call-update) | async-done | bytes 2097168 | tf_op jit(solution)/shard_map/all_gather | solution.py:44
  143.9 2.6 fusion.15
  146.7 86.8 %all-gather.14.cloned.1.call-done = bf16[2048,256]{1,0:T(8,128)(2,1)} async-done(((bf16[32,256]{1,0:T(8,128)(2,1)}), bf16[2048,256]{1,0:T(8,128)(2,1)}) %all-gather.14.cloned.1.call-update) | async-done | bytes 1048592 | tf_op jit(solution)/shard_map/all_gather | solution.py:48
  233.5 2.6 multiply_reduce_fusion
  236.2 1.2 fusion.14
  237.3 2.5 convolution_convert_fusion.1
  240.6 75.9 %all-gather.12.cloned.1.call-done = bf16[2048,256]{1,0:T(8,128)(2,1)} async-done(((bf16[32,256]{1,0:T(8,128)(2,1)}), bf16[2048,256]{1,0:T(8,128)(2,1)}) %all-gather.12.cloned.1.call-update) | async-done | bytes 1048592 | tf_op jit(solution)/shard_map/all_gather | solution.py:47
  316.5 2.6 multiply_reduce_fusion.1
  319.1 42.5 %all-gather.2 = bf16[64,2,256]{2,1,0:T(2,128)(2,1)S(1)} all-gather(bf16[1,2,256]{2,1,0:T(2,128)(2,1)S(1)} %bitcast.68), channel_id=3, replica_groups=mesh['ctx'=64,'tp'=8] {'ctx'}, dimensions={0}, use_global_device_ids=true | all-gather | bytes 66560 | tf_op jit(solution)/shard_map/all_gather | solution.py:12
  361.6 1.1 fusion.3
  362.7 2.1 select_reduce_fusion
  364.8 1.5 fusion
  366.4 40.4 %all-gather.20.cloned.1.call-done = bf16[128,256,128]{2,1,0:T(8,128)(2,1)} async-done(((bf16[2,256,128]{2,1,0:T(8,128)(2,1)}), bf16[128,256,128]{2,1,0:T(8,128)(2,1)}) %all-gather.20.cloned.1.call-update) | async-done | bytes 8388624 | tf_op jit(solution)/shard_map/all_gather | solution.py:12
  406.8 1.2 while.12
  406.8 0.9 convert_add_fusion.4
  408.0 1.0 fusion.11
  409.0 1.2 fusion.6
  410.2 78.5 %all-gather.18.cloned.1.call-done = bf16[256,2048]{0,1:T(8,128)(2,1)} async-done(((bf16[256,32]{0,1:T(8,128)(2,1)}), bf16[256,2048]{0,1:T(8,128)(2,1)}) %all-gather.18.cloned.1.call-update) | async-done | bytes 1048592 | tf_op jit(solution)/shard_map/all_gather | solution.py:108
  488.7 3.3 convolution_convert_fusion
  492.1 37.5 %reduce-scatter.2.cloned.1.call-done = bf16[512,256]{1,0:T(8,128)(2,1)} async-done(((bf16[512,2048]{1,0:T(8,128)(2,1)}), bf16[512,256]{1,0:T(8,128)(2,1)}) %reduce-scatter.2.cloned.1.call-update) | async-done | bytes 262160 | tf_op jit(solution)/shard_map/reduce_scatter | solution.py:110
  (21 shorter events, 1.6 us)
Async XLA Ops:
  6.5 229.6 %copy-start = (f32[2,256,128]{2,1,0:T(8,128)S(1)}, f32[2,256,128]{2,1,0:T(8,128)}, u32[]{:S(2)}) copy-start(f32[2,256,128]{2,1,0:T(8,128)} %param.12) | copy-start | bytes 786436
  6.5 92.6 %all-gather.16.cloned.1.call-start = ((), (), s32[]{:S(2)}) async-start(), calls=%async_computation.4 | async-start | bytes 1064960 | tf_op jit(solution)/shard_map/all_gather | solution.py:49
  7.3 136.7 %all-gather.10.cloned.1.call-start = ((), (), s32[]{:S(2)}) async-start(), calls=%async_computation.1 | async-start | bytes 2359296 | tf_op jit(solution)/shard_map/all_gather | solution.py:44
  8.0 225.5 %all-gather.14.cloned.1.call-start = ((), (), s32[]{:S(2)}) async-start(), calls=%async_computation.3 | async-start | bytes 1064960 | tf_op jit(solution)/shard_map/all_gather | solution.py:48
  8.7 307.8 %all-gather.12.cloned.1.call-start = ((), (), s32[]{:S(2)}) async-start(), calls=%async_computation.2 | async-start | bytes 1064960 | tf_op jit(solution)/shard_map/all_gather | solution.py:47
  9.3 397.4 %all-gather.20.cloned.1.call-start = ((), (), s32[]{:S(2)}) async-start(), calls=%async_computation.7 | async-start | bytes 8519680 | tf_op jit(solution)/shard_map/all_gather | solution.py:12
  239.9 248.8 %all-gather.18.cloned.1.call-start = ((), (), s32[]{:S(2)}) async-start(), calls=%async_computation.5 | async-start | bytes 1064960 | tf_op jit(solution)/shard_map/all_gather | solution.py:108
  240.5 289.1 %reduce-scatter.2.cloned.1.call-start = ((), (), s32[]{:S(2)}) async-start(), calls=%async_computation.6 | async-start | bytes 2359296 | tf_op jit(solution)/shard_map/reduce_scatter | solution.py:110
Sparse Core Ops, SparseCore 0:
  10.7 88.3 all-gather.15
  101.2 42.7 all-gather.9
  147.3 86.1 all-gather.13
  236.7 79.7 all-gather.11
  319.7 87.0 all-gather.19
  410.0 78.6 all-gather.17
  492.2 37.3 reduce-scatter.1
where the time goes:
time: 541 us; the launch traced here: 536 us
  waiting for transfers between devices  457 us (84%)
  blocking collectives  42.5 us (8%)
  matrix products  21.8 us (4%)
  between operations  13.6 us (3%)
    all_gather x1, waiting for transfers between devices, body(): lax.all_gather(w_value, 'ctx', axis=0, tiled=True)  89.8 us
    all_gather x1, waiting for transfers between devices, body(): lax.all_gather(w_key, 'ctx', axis=0, tiled=True)  86.8 us
    all_gather x1, waiting for transfers between devices, body(): lax.all_gather(w_out, 'ctx', axis=1, tiled=True)  78.5 us
    all_gather x1, waiting for transfers between devices, body(): lax.all_gather(w_query, 'ctx', axis=0, tiled=True)  75.9 us
    all_gather x1, waiting for transfers between devices, body(): whole = lax.all_gather(tokens, 'tp', axis=1, tiled=True)  44.8 us
    all_gather x1, blocking collectives, carried_in(): lax.all_gather(a.astype(kind), axis)  42.5 us
    all_gather x1, waiting for transfers between devices, carried_in(): lax.all_gather(a.astype(kind), axis)  40.4 us
    reduce_scatter x1, waiting for transfers between devices, body(): lax.psum_scatter(terms.astype(jnp.bfloat16), 'tp', scatter_dimension=1, t...  37.5 us
  transfers between devices with their start and end apart: 7, of which 7 were waited for; matrix products, arithmetic and copies ran while one was open for 4% of the time, Pallas kernels for 0%

commit v1 on v0

v1 whole, which is shorter than its diff:
```python
import jax
import jax.numpy as jnp
from jax import lax
from jax.experimental import pallas as pl
from jax.experimental.pallas import tpu as pltpu
from jax.sharding import PartitionSpec as P

NX, NZ, NC, NY = 4, 8, 2, 8
GROUP = NZ * NC
TOK = 512
HALF = 256
WIDTH = 256
DH = 128
MF = 256
SHARD = 32
SLICE = 16
SENDS = 128
BF = jnp.bfloat16
F32 = jnp.float32
NT = (((1,), (1,)), ((), ()))
TN = (((0,), (0,)), ((), ()))


def kernel(
    tok_ref, wq_ref, wk_ref, wv_ref, feat_ref, wo_ref, out_ref,
    tok, w, kv, q, vaug, phik, phiq, fcat, nd, ssend, precv, excl, tot, psend, pfx, attn,
    rs_send, rs_recv,
    ssem, tok_sem, z_sem, x_sem, sib_sem, a_sem, b_sem, c_sem, rs_sem,
):
    ctx = lax.axis_index("ctx")
    y = lax.axis_index("tp")
    c = lax.rem(ctx, NC)
    z = lax.rem(lax.div(ctx, NC), NZ)
    x = lax.div(ctx, GROUP)
    me16 = lax.rem(ctx, GROUP)

    def at(xx, zz, cc):
        return {"ctx": (xx * NZ + zz) * NC + cc, "tp": y}

    def at_y(yy):
        return {"ctx": ctx, "tp": yy}

    def turn(v, by, n):
        return lax.rem(v + (by % n), n)

    def peer16(d):
        return turn(me16, d, GROUP)

    def dev16(p):
        return {"ctx": x * GROUP + p, "tp": y}

    ups = [at_y(turn(y, 1, NY)), at_y(turn(y, -1, NY))]
    sides = [at(turn(x, 1, NX), z, c), at(turn(x, -1, NX), z, c)]
    sib = at(x, z, 1 - c)

    barrier = pltpu.get_barrier_semaphore()
    greeted = (
        [dev16(peer16(d)) for d in range(1, GROUP)]
        + [at(turn(x, d, NX), z, c) for d in range(1, NX)]
        + ups
    )
    for p in greeted:
        pl.semaphore_signal(barrier, inc=1, device_id=p, device_id_type=pl.DeviceIdType.MESH)

    tok[y] = tok_ref[...]
    w[x, z, c, 0] = wk_ref[...]
    w[x, z, c, 1] = wv_ref[...]
    w[x, z, c, 2] = wq_ref[...]
    rows = lax.broadcasted_iota(jnp.int32, (SHARD, SHARD), 0)
    cols = lax.broadcasted_iota(jnp.int32, (SHARD, SHARD), 1)
    eye = (rows == cols).astype(F32).astype(BF)
    w[x, z, c, 3] = lax.dot_general(eye, wo_ref[...], NT, preferred_element_type=F32).astype(BF)

    pl.semaphore_wait(barrier, len(greeted))

    sends = []

    def send(src, dst, rsem, dev):
        copy = pltpu.make_async_remote_copy(
            src_ref=src, dst_ref=dst, send_sem=ssem.at[len(sends)], recv_sem=rsem,
            device_id=dev, device_id_type=pl.DeviceIdType.MESH,
        )
        copy.start()
        sends.append(copy)

    def recv(dst, rsem):
        pltpu.make_async_copy(dst, dst, rsem).wait()

    def tok_owner(d, step):
        return turn(y, -step if d == 0 else step, NY)

    def tok_part(owner, r):
        return tok.at[owner, pl.ds(r * HALF, HALF)]

    def tok_send(d, step, r):
        part = tok_part(tok_owner(d, step), r)
        send(part, part, tok_sem.at[d, step, r], ups[d])

    def tok_recv(d, step, r):
        recv(tok_part(tok_owner(d, step + 1), r), tok_sem.at[d, step, r])

    def w_part(xx, zs, cc, part):
        return w.at[xx, zs, cc, pl.ds(2 * part, 2)]

    def z_send(part):
        own = w_part(x, z, c, part)
        for d in (4, 3, 5, 2, 6, 1, 7):
            send(own, own, z_sem.at[part, z], at(x, turn(z, d, NZ), c))

    def z_recv(part):
        for d in (1, 7, 2, 6, 3, 5, 4):
            zz = turn(z, d, NZ)
            recv(w_part(x, zz, c, part), z_sem.at[part, zz])

    every = pl.ds(0, NZ)
    halves = (pl.ds(0, NZ // 2), pl.ds(NZ // 2, NZ // 2))

    def x_start(part):
        block = w_part(x, every, c, part)
        for d in range(2):
            send(block, block, x_sem.at[part, d], sides[d])

    def sib_send(part, i, xx, zs):
        block = w_part(xx, zs, c, part)
        send(block, block, sib_sem.at[part, i], sib)

    def x_near(part):
        for d in range(2):
            xx = turn(x, -1 if d == 0 else 1, NX)
            recv(w_part(xx, every, c, part), x_sem.at[part, d])
            half = w_part(xx, halves[d], c, part)
            send(half, half, x_sem.at[part, 2 + d], sides[d])
            sib_send(part, 1 + d, xx, every)

    def x_far(part):
        xx = turn(x, 2, NX)
        for d in range(2):
            recv(w_part(xx, halves[d], c, part), x_sem.at[part, 2 + d])
            sib_send(part, 3 + d, xx, halves[d])

    def sib_recv(part):
        o = 1 - c
        blocks = [
            (x, every), (turn(x, -1, NX), every), (turn(x, 1, NX), every),
            (turn(x, 2, NX), halves[0]), (turn(x, 2, NX), halves[1]),
        ]
        for i, (xx, zs) in enumerate(blocks):
            recv(w_part(xx, zs, o, part), sib_sem.at[part, i])

    for r in range(2):
        for d in range(2):
            tok_send(d, 0, r)
    z_send(0)
    z_send(1)

    for h in range(2):
        f = feat_ref[h]
        hi = f.astype(BF)
        lo = (f - hi.astype(F32)).astype(BF)
        fcat[h] = jnp.concatenate([hi, hi, lo], axis=1)

    z_recv(0)
    x_start(0)
    sib_send(0, 0, x, every)

    for r in range(2):
        for d in range(2):
            tok_recv(d, 0, r)
            tok_send(d, 1, r)

    z_recv(1)
    sib_send(1, 0, x, every)
    x_near(0)
    x_start(1)

    for r in range(2):
        for d in range(2):
            tok_recv(d, 1, r)
            tok_send(d, 2, r)

    x_far(0)
    x_near(1)

    tok_recv(0, 2, 0)
    tok_send(0, 3, 0)
    tok_recv(1, 2, 1)
    tok_send(1, 3, 1)

    sib_recv(0)

    def w_rows(s, k):
        return w[lax.div(s, 2), pl.ds(lax.rem(s, 2) * 4, 4), :, k].reshape(WIDTH, WIDTH)

    def kv_term(s, r):
        t = tok[s, pl.ds(r * HALF, HALF)]
        k = jnp.dot(t, w_rows(s, 0), preferred_element_type=F32)
        v = jnp.dot(t, w_rows(s, 1), preferred_element_type=F32)
        return k, v

    def kv_add(s):
        for r in range(2):
            k, v = kv_term(s, r)
            kv[0, pl.ds(r * HALF, HALF)] += k
            kv[1, pl.ds(r * HALF, HALF)] += v

    kv[...] = jnp.zeros_like(kv)

    @pl.loop(0, 5)
    def _(i):
        kv_add(lax.rem(y + i + (NY - 2), NY))

    x_far(1)

    tok_recv(0, 2, 1)
    tok_recv(1, 2, 0)

    @pl.loop(0, 2)
    def _(i):
        kv_add(lax.rem(y + 3 + 2 * i, NY))

    tok_recv(0, 3, 0)
    tok_recv(1, 3, 1)
    kv_add(turn(y, 4, NY))

    def positive(p, h):
        s = p * (DH ** -0.25)
        half_square = 0.5 * jnp.sum(s * s, axis=-1, keepdims=True)
        hi = s.astype(BF)
        lo = (s - hi.astype(F32)).astype(BF)
        logits = lax.dot_general(
            jnp.concatenate([hi, lo, hi], axis=1), fcat[h], NT, preferred_element_type=F32
        )
        return jnp.exp(logits - half_square).astype(BF)

    lane = lax.broadcasted_iota(jnp.int32, (MF, DH), 1)
    sums = []
    for h in range(2):
        head = pl.ds(h * DH, DH)
        vaug[h, :, pl.ds(0, DH)] = kv[1, :, head].astype(BF)
        vaug[h, :, pl.ds(DH, DH)] = jnp.ones((TOK, DH), BF)
        phik[h] = positive(kv[0, :, head], h)
        s = lax.dot_general(phik[h], vaug[h], TN, preferred_element_type=F32)
        ssend[:, head] = s[:, :DH].astype(BF)
        sums.append(s[:, DH:])
    ssend[:, pl.ds(2 * DH, DH)] = jnp.where(lane < DH // 2, sums[0], sums[1]).astype(BF)

    for d in range(1, GROUP):
        p = peer16(d)
        send(
            ssend.at[pl.ds(pl.multiple_of(p * SLICE, SLICE), SLICE)],
            precv.at[me16], a_sem.at[me16], dev16(p),
        )
    precv[me16] = ssend[pl.ds(pl.multiple_of(me16 * SLICE, SLICE), SLICE)]

    sib_recv(1)

    @pl.loop(0, NY)
    def _(s):
        for r in range(2):
            t = tok[s, pl.ds(r * HALF, HALF)]
            term = jnp.dot(t, w_rows(s, 2), preferred_element_type=F32)
            rows_r = pl.ds(r * HALF, HALF)

            @pl.when(s == 0)
            def _():
                q[rows_r] = term

            @pl.when(s > 0)
            def _():
                q[rows_r] += term

    for d in range(1, GROUP):
        p = peer16(d)
        recv(precv.at[p], a_sem.at[p])
    run = jnp.zeros((SLICE, 3 * DH), F32)
    for i in range(GROUP):
        excl[i] = run
        run = run + precv[i].astype(F32)
    tot[x] = run
    for d in range(1, NX):
        send(tot.at[x], tot.at[x], b_sem.at[x], at(turn(x, d, NX), z, c))

    def local(h):
        head = pl.ds(h * DH, DH)
        phiq[h] = positive(q[:, head], h)
        for r in range(2):
            rows_r = pl.ds(r * HALF, HALF)
            upto = (r + 1) * HALF
            sc = lax.dot_general(
                phiq[h, rows_r], phik[h, pl.ds(0, upto)], NT, preferred_element_type=F32
            )
            row = lax.broadcasted_iota(jnp.int32, (HALF, upto), 0) + r * HALF
            col = lax.broadcasted_iota(jnp.int32, (HALF, upto), 1)
            sc = jnp.where(col <= row, sc, 0.0).astype(BF)
            nd[h, rows_r] = jnp.dot(sc, vaug[h, pl.ds(0, upto)], preferred_element_type=F32)

    local(0)

    for d in range(1, NX):
        xx = turn(x, d, NX)
        recv(tot.at[xx], b_sem.at[xx])
    base = jnp.zeros((SLICE, 3 * DH), F32)
    for i in range(NX):
        base = base + jnp.where(i < x, tot[i], 0.0)
    for i in range(GROUP):
        psend[i] = (excl[i] + base).astype(BF)
    for d in range(1, GROUP):
        p = peer16(d)
        send(psend.at[p], pfx.at[me16], c_sem.at[me16], dev16(p))
    pfx[me16] = psend[me16]

    local(1)

    for d in range(1, GROUP):
        p = peer16(d)
        recv(pfx.at[p], c_sem.at[p])

    prefix = pfx[...].reshape(MF, 3 * DH)
    pick_r = lax.broadcasted_iota(jnp.int32, (DH, 2 * DH), 0)
    pick_c = lax.broadcasted_iota(jnp.int32, (DH, 2 * DH), 1)
    pick = (pick_r == jnp.where(pick_c < DH, 0, DH // 2)).astype(F32).astype(BF)
    spread = jnp.dot(prefix[:, 2 * DH :], pick, preferred_element_type=F32).astype(BF)
    for h in range(2):
        state = jnp.concatenate(
            [prefix[:, h * DH : (h + 1) * DH], spread[:, h * DH : (h + 1) * DH]], axis=1
        )
        full = nd[h] + jnp.dot(phiq[h], state, preferred_element_type=F32)
        attn[:, pl.ds(h * DH, DH)] = (full[:, :DH] / full[:, DH:]).astype(BF)

    def share(dest, r):
        return lax.dot_general(
            attn[pl.ds(r * HALF, HALF)], w_rows(dest, 3), NT, preferred_element_type=F32
        )

    def rs_item(d, step, r, first):
        dest = turn(y, (4 - step) if d == 0 else (step - 4), NY)
        value = share(dest, r)
        if not first:
            recv(rs_recv.at[d, step - 1, r], rs_sem.at[d, step - 1, r])
            value = value + rs_recv[d, step - 1, r].astype(F32)
        rs_send[d, step, r] = value.astype(BF)
        send(rs_send.at[d, step, r], rs_recv.at[d, step, r], rs_sem.at[d, step, r], ups[d])

    for d in range(2):
        rs_item(d, 0, d, True)
    for step in range(1, 4):
        for k in range(2):
            for d in range(2):
                rs_item(d, step, (1 - d) if k == 0 else d, step == 1 and k == 0)
    for r in range(2):
        value = share(y, r)
        for d in range(2):
            recv(rs_recv.at[d, 3, r], rs_sem.at[d, 3, r])
            value = value + rs_recv[d, 3, r].astype(F32)
        out_ref[pl.ds(r * HALF, HALF)] = value.astype(BF)

    for copy in sends:
        copy.wait_send()


def body(tokens, w_query, w_key, w_value, features, w_out):
    vmem = pl.BlockSpec(memory_space=pltpu.VMEM)
    dma = pltpu.SemaphoreType.DMA
    return pl.pallas_call(
        kernel,
        out_shape=jax.ShapeDtypeStruct((TOK, WIDTH), BF),
        in_specs=[vmem] * 6,
        out_specs=vmem,
        scratch_shapes=[
            pltpu.VMEM((NY, TOK, WIDTH), BF),
            pltpu.VMEM((NX, NZ, NC, 4, SHARD, WIDTH), BF),
            pltpu.VMEM((2, TOK, WIDTH), F32),
            pltpu.VMEM((TOK, WIDTH), F32),
            pltpu.VMEM((2, TOK, 2 * DH), BF),
            pltpu.VMEM((2, TOK, MF), BF),
            pltpu.VMEM((2, TOK, MF), BF),
            pltpu.VMEM((2, MF, 3 * DH), BF),
            pltpu.VMEM((2, TOK, 2 * DH), F32),
            pltpu.VMEM((MF, 3 * DH), BF),
            pltpu.VMEM((GROUP, SLICE, 3 * DH), BF),
            pltpu.VMEM((GROUP, SLICE, 3 * DH), F32),
            pltpu.VMEM((NX, SLICE, 3 * DH), F32),
            pltpu.VMEM((GROUP, SLICE, 3 * DH), BF),
            pltpu.VMEM((GROUP, SLICE, 3 * DH), BF),
            pltpu.VMEM((TOK, 2 * DH), BF),
            pltpu.VMEM((2, 4, 2, HALF, WIDTH), BF),
            pltpu.VMEM((2, 4, 2, HALF, WIDTH), BF),
            dma((SENDS,)),
            dma((2, 4, 2)),
            dma((2, NZ)),
            dma((2, 4)),
            dma((2, 5)),
            dma((GROUP,)),
            dma((NX,)),
            dma((GROUP,)),
            dma((2, 4, 2)),
        ],
        compiler_params=pltpu.CompilerParams(
            collective_id=0, has_side_effects=True, vmem_limit_bytes=48 * 1024 * 1024
        ),
    )(tokens, w_query, w_key, w_value, features, w_out)


def solution(mesh):
    return jax.shard_map(
        body,
        mesh=mesh,
        in_specs=(
            P("ctx", "tp"),
            P("ctx", "tp"),
            P("ctx", "tp"),
            P("ctx", "tp"),
            P("tp", None, None),
            P("tp", "ctx"),
        ),
        out_specs=P("ctx", "tp"),
        check_vma=False,
    )
```

time: 541 us -> 92.9 us (0.17)
  waiting for transfers between devices: 457 us -> 0 us
  Pallas kernels: 0 us -> 89.1 us
  blocking collectives: 42.5 us -> 0 us
  matrix products: 21.8 us -> 0 us
  between operations: 13.6 us -> 0.04 us
    all_gather x6 -> x0, waiting for transfers between devices: 416 us -> none  [the longest x1 89.8 us: body(): lax.all_gather(w_value, 'ctx', axis=0, tiled=True)]
    pallas_call x0 -> x1, Pallas kernels: none -> 89.1 us  [body(): pl.pallas_call(kernel, out_shape=jax.ShapeDtypeStruct((TOK, WIDTH), BF),...]
    all_gather x1 -> x0, blocking collectives: 42.5 us -> none  [carried_in(): lax.all_gather(a.astype(kind), axis)]
    reduce_scatter x1 -> x0, waiting for transfers between devices: 37.5 us -> none  [body(): lax.psum_scatter(terms.astype(jnp.bfloat16), 'tp', scatter_dimension=1, t...]
    dot_general x11 -> x0, matrix products: 21.8 us -> none  [the longest x1 3.32 us: body(): jnp.dot(attn, lax.all_gather(w_out, 'ctx', axis=1, tiled=True), preferred...]
  transfers between devices with their start and end apart: 7 -> 0, of which waited for: 7 -> 0; matrix products, arithmetic and copies ran while one was open for 4% -> 0% of each run, Pallas kernels for 0% -> 0%
where the time goes in v1:
time: 92.9 us; the launch traced here: 92.6 us
  Pallas kernels  89.1 us (96%)
  local copies, waits for them, and re-layouts  3.48 us (4%)
    pallas_call x1, Pallas kernels, body(): pl.pallas_call(kernel, out_shape=jax.ShapeDtypeStruct((TOK, WIDTH), BF),...  89.1 us
    unnamed x12, local copies, waits for them, and re-layouts  3.48 us

profile of v1, /device:TPU:1, one launch (start us, length us, event | category | flops | bytes accessed | tf_op | source)
XLA Modules:
  0.0 92.6 jit_solution(17991898646417283209)
XLA Ops:
  0.0 0.0 copy-start.4
  0.0 0.0 copy-start.3
  0.0 0.0 copy-start.2
  0.0 0.9 copy.7.wo_ref
  0.9 0.0 copy-done.4
  0.9 0.0 copy-done.3
  0.9 0.0 copy-done.2
  0.9 0.0 copy-start
  0.9 0.9 %copy-done = bf16[512,256]{1,0:T(8,128)(2,1)S(1)} copy-done((bf16[512,256]{1,0:T(8,128)(2,1)S(1)}, bf16[512,256]{1,0:T(8,128)(2,1)}, u32[]{:S(2)}) %copy-start) | copy-done | bytes 262168
  1.9 0.0 copy-start.1
  1.9 0.9 %copy-done.1 = f32[2,256,128]{2,1,0:T(8,128)S(1)} copy-done((f32[2,256,128]{2,1,0:T(8,128)S(1)}, f32[2,256,128]{2,1,0:T(8,128)}, u32[]{:S(2)}) %copy-start.1) | copy-done | bytes 262168
  2.8 89.1 %shard_map.64 = bf16[512,256]{1,0:T(8,128)(2,1)S(1)} custom-call(bf16[512,256]{1,0:T(8,128)(2,1)S(1)} %copy-done, bf16[32,256]{1,0:T(8,128)(2,1)S(1)} %copy-done.2, bf16[32,256]{1,0:T(8,128)(2,1)S(1)} %copy-done.3, bf16[32,256]{1,0:T(8,128)(2,1)S(1)} %copy-done.4, f32[2,256,128]{2,1,0:T(8,128)S(1)} %copy-done.1, bf16[256,32]{1,0:T(8,128)(2,1)S(1)} %copy.7.wo_ref), custom_call_target="tpu_custom_call" | custom-call | tf_op jit(solution)/shard_map/pallas_call | solution.py:364
  91.9 0.7 copy.9
Async XLA Ops:
  0.0 0.9 copy-start.4
  0.0 0.9 copy-start.3
  0.0 0.9 copy-start.2
  0.9 1.0 %copy-start = (bf16[512,256]{1,0:T(8,128)(2,1)S(1)}, bf16[512,256]{1,0:T(8,128)(2,1)}, u32[]{:S(2)}) copy-start(bf16[512,256]{1,0:T(8,128)(2,1)} %tok_ref.1) | copy-start | bytes 786436
  1.9 0.9 %copy-start.1 = (f32[2,256,128]{2,1,0:T(8,128)S(1)}, f32[2,256,128]{2,1,0:T(8,128)}, u32[]{:S(2)}) copy-start(f32[2,256,128]{2,1,0:T(8,128)} %feat_ref.1) | copy-start | bytes 786436

commit v2 on v1

v2 whole, which is shorter than its diff:
```python
import jax
import jax.numpy as jnp
from jax import lax
from jax.experimental import pallas as pl
from jax.experimental.pallas import tpu as pltpu
from jax.sharding import PartitionSpec as P

NX, NZ, NC, NY = 4, 8, 2, 8
GROUP = NZ * NC
TOK = 512
HALF = 256
WIDTH = 256
DH = 128
MF = 256
SHARD = 32
SLICE = 16
SENDS = 128
BF = jnp.bfloat16
F32 = jnp.float32
NT = (((1,), (1,)), ((), ()))
TN = (((0,), (0,)), ((), ()))


def kernel(
    tok_ref, wq_ref, wk_ref, wv_ref, feat_ref, wo_ref, out_ref,
    tok, w, kv, q, vaug, phik, phiq, feat, fcat, nd, ssend, srecv, tsend, arecv, excl, tot,
    psend, pfx, fsend, frecv, own, attn, rs_send, rs_recv,
    loc_sem, ssem, tok_sem, z_sem, x_sem, sib_sem, a_sem, b_sem, c_sem, j_sem, rs_sem,
):
    ctx = lax.axis_index("ctx")
    y = lax.axis_index("tp")
    c = lax.rem(ctx, NC)
    z = lax.rem(lax.div(ctx, NC), NZ)
    x = lax.div(ctx, GROUP)

    def at(xx, zz, cc):
        return {"ctx": (xx * NZ + zz) * NC + cc, "tp": y}

    def at_y(yy):
        return {"ctx": ctx, "tp": yy}

    def turn(v, by, n):
        return lax.rem(v + (by % n), n)

    ups = [at_y(turn(y, 1, NY)), at_y(turn(y, -1, NY))]
    sides = [at(turn(x, 1, NX), z, c), at(turn(x, -1, NX), z, c)]
    sib = at(x, z, 1 - c)

    barrier = pltpu.get_barrier_semaphore()
    greeted = (
        ups
        + [at(x, turn(z, d, NZ), c) for d in (4, 3, 5, 2, 6, 1, 7)]
        + [at(turn(x, d, NX), z, c) for d in (2, 1, 3)]
        + [sib]
    )
    for p in greeted:
        pl.semaphore_signal(barrier, inc=1, device_id=p, device_id_type=pl.DeviceIdType.MESH)

    loads = [
        pltpu.make_async_copy(src, dst, loc_sem.at[i])
        for i, (src, dst) in enumerate([
            (tok_ref, tok.at[y]),
            (wk_ref, w.at[x, z, c, 0]),
            (wv_ref, w.at[x, z, c, 1]),
            (wq_ref, w.at[x, z, c, 2]),
            (wo_ref, w.at[x, z, c, 3]),
            (feat_ref, feat),
        ])
    ]
    for copy in loads:
        copy.start()
    for copy in loads:
        copy.wait()

    for h in range(2):
        f = feat[h]
        hi = f.astype(BF)
        lo = (f - hi.astype(F32)).astype(BF)
        fcat[h] = jnp.concatenate([hi, hi, lo], axis=1)

    pl.semaphore_wait(barrier, len(greeted))

    sends = []

    def send(src, dst, rsem, dev):
        copy = pltpu.make_async_remote_copy(
            src_ref=src, dst_ref=dst, send_sem=ssem.at[len(sends)], recv_sem=rsem,
            device_id=dev, device_id_type=pl.DeviceIdType.MESH,
        )
        copy.start()
        sends.append(copy)

    def recv(dst, rsem):
        pltpu.make_async_copy(dst, dst, rsem).wait()

    def tok_owner(d, step):
        return turn(y, -step if d == 0 else step, NY)

    def tok_part(owner, r):
        return tok.at[owner, pl.ds(r * HALF, HALF)]

    def tok_send(d, step, r):
        part = tok_part(tok_owner(d, step), r)
        send(part, part, tok_sem.at[d, step, r], ups[d])

    def tok_recv(d, step, r):
        recv(tok_part(tok_owner(d, step + 1), r), tok_sem.at[d, step, r])

    spans = (pl.ds(0, 2), pl.ds(2, 1), pl.ds(3, 1))

    def w_part(xx, zs, cc, part):
        return w.at[xx, zs, cc, spans[part]]

    def z_send(part):
        mine = w_part(x, z, c, part)
        for d in (4, 3, 5, 2, 6, 1, 7):
            send(mine, mine, z_sem.at[part, z], at(x, turn(z, d, NZ), c))

    def z_recv(part):
        for d in (1, 7, 2, 6, 3, 5, 4):
            zz = turn(z, d, NZ)
            recv(w_part(x, zz, c, part), z_sem.at[part, zz])

    every = pl.ds(0, NZ)
    halves = (pl.ds(0, NZ // 2), pl.ds(NZ // 2, NZ // 2))

    def sib_send(part, i, xx, zs):
        block = w_part(xx, zs, c, part)
        send(block, block, sib_sem.at[part, i], sib)

    def x_start(part):
        for i in range(2):
            for d in range(2):
                half = w_part(x, halves[d if i == 0 else 1 - d], c, part)
                send(half, half, x_sem.at[part, 2 * d + i], sides[d])
        sib_send(part, 0, x, every)

    def x_near(part, i):
        for d in range(2):
            xx = turn(x, -1 if d == 0 else 1, NX)
            zs = halves[d if i == 0 else 1 - d]
            half = w_part(xx, zs, c, part)
            recv(half, x_sem.at[part, 2 * d + i])
            if i == 0:
                send(half, half, x_sem.at[part, 4 + d], sides[d])
            sib_send(part, 1 + 2 * d + i, xx, zs)

    def x_far(part):
        xx = turn(x, 2, NX)
        for d in range(2):
            recv(w_part(xx, halves[d], c, part), x_sem.at[part, 4 + d])
            sib_send(part, 5 + d, xx, halves[d])

    def sib_recv(part):
        o = 1 - c
        recv(w_part(x, every, o, part), sib_sem.at[part, 0])
        for d in range(2):
            for i in range(2):
                xx = turn(x, -1 if d == 0 else 1, NX)
                recv(w_part(xx, halves[d if i == 0 else 1 - d], o, part), sib_sem.at[part, 1 + 2 * d + i])
            recv(w_part(turn(x, 2, NX), halves[d], o, part), sib_sem.at[part, 5 + d])

    for r in range(2):
        for d in range(2):
            tok_send(d, 0, r)
    z_send(0)

    def tok_pass(step, r):
        for d in range(2):
            tok_recv(d, step, r)
            tok_send(d, step + 1, r)

    tok_pass(0, 0)
    tok_pass(0, 1)
    z_recv(0)
    x_start(0)
    z_send(1)
    z_send(2)
    tok_pass(1, 0)
    tok_pass(1, 1)
    x_near(0, 0)
    tok_recv(0, 2, 0)
    tok_send(0, 3, 0)
    x_near(0, 1)
    z_recv(1)
    x_start(1)
    tok_recv(1, 2, 1)
    tok_send(1, 3, 1)
    x_far(0)
    z_recv(2)
    sib_recv(0)

    def w_rows(s, k):
        return w[lax.div(s, 2), pl.ds(lax.rem(s, 2) * 4, 4), :, k].reshape(WIDTH, WIDTH)

    def kv_term(s, r):
        t = tok[s, pl.ds(r * HALF, HALF)]
        k = jnp.dot(t, w_rows(s, 0), preferred_element_type=F32)
        v = jnp.dot(t, w_rows(s, 1), preferred_element_type=F32)
        return k, v

    def kv_add(s):
        for r in range(2):
            k, v = kv_term(s, r)
            kv[0, pl.ds(r * HALF, HALF)] += k
            kv[1, pl.ds(r * HALF, HALF)] += v

    kv[...] = jnp.zeros_like(kv)

    @pl.loop(0, 5)
    def _(i):
        kv_add(lax.rem(y + i + (NY - 2), NY))

    x_near(1, 0)

    tok_recv(0, 2, 1)
    tok_recv(1, 2, 0)

    @pl.loop(0, 2)
    def _(i):
        kv_add(lax.rem(y + 3 + 2 * i, NY))

    tok_recv(0, 3, 0)
    tok_recv(1, 3, 1)
    kv_add(turn(y, 4, NY))

    def positive(p, h):
        s = p * (DH ** -0.25)
        half_square = 0.5 * jnp.sum(s * s, axis=-1, keepdims=True)
        hi = s.astype(BF)
        lo = (s - hi.astype(F32)).astype(BF)
        logits = lax.dot_general(
            jnp.concatenate([hi, lo, hi], axis=1), fcat[h], NT, preferred_element_type=F32
        )
        return jnp.exp(logits - half_square).astype(BF)

    def key_sums(h):
        head = pl.ds(pl.multiple_of(h * DH, DH), DH)
        vaug[h, :, pl.ds(0, DH)] = kv[1, :, head].astype(BF)
        vaug[h, :, pl.ds(DH, DH)] = jnp.ones((TOK, DH), BF)
        phik[h] = positive(kv[0, :, head], h)
        return lax.dot_general(phik[h], vaug[h], TN, preferred_element_type=F32)

    ssend[...] = key_sums(1 - c).astype(BF)
    send(ssend, srecv, j_sem.at[0], sib)
    own[...] = key_sums(c).astype(BF).astype(F32)
    recv(srecv, j_sem.at[0])
    chip = own[...] + srecv[...].astype(F32)
    lane = lax.broadcasted_iota(jnp.int32, (NZ, SLICE, DH), 2)
    norm = chip[:, DH:].reshape(NZ, 2, SLICE, DH)
    tsend[:, pl.ds(0, 2 * SLICE)] = chip[:, :DH].reshape(NZ, 2 * SLICE, DH).astype(BF)
    tsend[:, pl.ds(2 * SLICE, SLICE)] = jnp.where(lane < DH // 2, norm[:, 0], norm[:, 1]).astype(BF)

    for d in (4, 3, 5, 2, 6, 1, 7):
        zz = turn(z, d, NZ)
        send(tsend.at[zz], arecv.at[z], a_sem.at[z], at(x, zz, c))
    arecv[z] = tsend[z]

    x_near(1, 1)
    x_start(2)
    x_far(1)
    sib_recv(1)

    @pl.loop(0, NY)
    def _(s):
        for r in range(2):
            t = tok[s, pl.ds(r * HALF, HALF)]
            term = jnp.dot(t, w_rows(s, 2), preferred_element_type=F32)
            rows_r = pl.ds(r * HALF, HALF)

            @pl.when(s == 0)
            def _():
                q[rows_r] = term

            @pl.when(s > 0)
            def _():
                q[rows_r] += term

    for h in range(2):
        phiq[h] = positive(q[:, pl.ds(h * DH, DH)], h)

    for d in (1, 7, 2, 6, 3, 5, 4):
        zz = turn(z, d, NZ)
        recv(arecv.at[zz], a_sem.at[zz])
    run = jnp.zeros((3 * SLICE, DH), F32)
    for i in range(NZ):
        excl[i] = run
        run = run + arecv[i].astype(F32)
    tot[x] = run.astype(BF)
    for d in (2, 1, 3):
        send(tot.at[x], tot.at[x], b_sem.at[x], at(turn(x, d, NX), z, c))

    def local(h):
        for r in range(2):
            rows_r = pl.ds(r * HALF, HALF)
            upto = (r + 1) * HALF
            sc = lax.dot_general(
                phiq[h, rows_r], phik[h, pl.ds(0, upto)], NT, preferred_element_type=F32
            )
            row = lax.broadcasted_iota(jnp.int32, (HALF, upto), 0) + r * HALF
            col = lax.broadcasted_iota(jnp.int32, (HALF, upto), 1)
            sc = jnp.where(col <= row, sc, 0.0).astype(BF)
            nd[h, rows_r] = jnp.dot(sc, vaug[h, pl.ds(0, upto)], preferred_element_type=F32)

    x_near(2, 0)
    local(0)

    for d in range(1, NX):
        xx = turn(x, d, NX)
        recv(tot.at[xx], b_sem.at[xx])
    base = jnp.zeros((3 * SLICE, DH), F32)
    for i in range(NX):
        base = base + jnp.where(i < x, tot[i].astype(F32), 0.0)
    for i in range(NZ):
        psend[i] = (excl[i] + base).astype(BF)
    for d in (4, 3, 5, 2, 6, 1, 7):
        zz = turn(z, d, NZ)
        send(psend.at[zz], pfx.at[z], c_sem.at[z], at(x, zz, c))
    pfx[z] = psend[z]

    x_near(2, 1)
    local(1)
    x_far(2)
    sib_recv(2)

    for d in (1, 7, 2, 6, 3, 5, 4):
        zz = turn(z, d, NZ)
        recv(pfx.at[zz], c_sem.at[zz])

    pick_r = lax.broadcasted_iota(jnp.int32, (DH, 2 * DH), 0)
    pick_c = lax.broadcasted_iota(jnp.int32, (DH, 2 * DH), 1)
    pick = (pick_r == jnp.where(pick_c < DH, 0, DH // 2)).astype(F32).astype(BF)
    spread = jnp.dot(
        pfx[:, pl.ds(2 * SLICE, SLICE)].reshape(NZ * SLICE, DH), pick, preferred_element_type=F32
    ).reshape(NZ, SLICE, 2 * DH)
    norm = jnp.stack([spread[:, :, :DH], spread[:, :, DH:]], axis=1).reshape(MF, DH)
    before = jnp.concatenate(
        [pfx[:, pl.ds(0, 2 * SLICE)].reshape(MF, DH).astype(F32), norm], axis=1
    )
    fsend[...] = (before + jnp.where(c == 0, own[...], 0.0)).astype(BF)
    send(fsend, frecv, j_sem.at[1], sib)
    state = (before + jnp.where(c == 0, 0.0, srecv[...].astype(F32))).astype(BF)

    def finish(h, state):
        full = nd[h] + jnp.dot(phiq[h], state, preferred_element_type=F32)
        head = pl.ds(pl.multiple_of(h * DH, DH), DH)
        attn[:, head] = (full[:, :DH] / full[:, DH:]).astype(BF)

    finish(c, state)
    recv(frecv, j_sem.at[1])
    finish(1 - c, frecv[...])

    def share(dest, r):
        return lax.dot_general(
            attn[pl.ds(r * HALF, HALF)], w_rows(dest, 3), NT, preferred_element_type=F32
        )

    def rs_item(d, step, r, first):
        dest = turn(y, (4 - step) if d == 0 else (step - 4), NY)
        value = share(dest, r)
        if not first:
            recv(rs_recv.at[d, step - 1, r], rs_sem.at[d, step - 1, r])
            value = value + rs_recv[d, step - 1, r].astype(F32)
        rs_send[d, step, r] = value.astype(BF)
        send(rs_send.at[d, step, r], rs_recv.at[d, step, r], rs_sem.at[d, step, r], ups[d])

    for d in range(2):
        rs_item(d, 0, d, True)
    for step in range(1, 4):
        for k in range(2):
            for d in range(2):
                rs_item(d, step, (1 - d) if k == 0 else d, step == 1 and k == 0)
    for r in range(2):
        value = share(y, r)
        for d in range(2):
            recv(rs_recv.at[d, 3, r], rs_sem.at[d, 3, r])
            value = value + rs_recv[d, 3, r].astype(F32)
        out_ref[pl.ds(r * HALF, HALF)] = value.astype(BF)

    for copy in sends:
        copy.wait_send()


def body(tokens, w_query, w_key, w_value, features, w_out):
    hbm = pl.BlockSpec(memory_space=pl.ANY)
    dma = pltpu.SemaphoreType.DMA
    return pl.pallas_call(
        kernel,
        out_shape=jax.ShapeDtypeStruct((TOK, WIDTH), BF),
        in_specs=[hbm] * 6,
        out_specs=pl.BlockSpec(memory_space=pltpu.VMEM),
        scratch_shapes=[
            pltpu.VMEM((NY, TOK, WIDTH), BF),
            pltpu.VMEM((NX, NZ, NC, 4, SHARD, WIDTH), BF),
            pltpu.VMEM((2, TOK, WIDTH), F32),
            pltpu.VMEM((TOK, WIDTH), F32),
            pltpu.VMEM((2, TOK, 2 * DH), BF),
            pltpu.VMEM((2, TOK, MF), BF),
            pltpu.VMEM((2, TOK, MF), BF),
            pltpu.VMEM((2, MF, DH), F32),
            pltpu.VMEM((2, MF, 3 * DH), BF),
            pltpu.VMEM((2, TOK, 2 * DH), F32),
            pltpu.VMEM((MF, 2 * DH), BF),
            pltpu.VMEM((MF, 2 * DH), BF),
            pltpu.VMEM((NZ, 3 * SLICE, DH), BF),
            pltpu.VMEM((NZ, 3 * SLICE, DH), BF),
            pltpu.VMEM((NZ, 3 * SLICE, DH), F32),
            pltpu.VMEM((NX, 3 * SLICE, DH), BF),
            pltpu.VMEM((NZ, 3 * SLICE, DH), BF),
            pltpu.VMEM((NZ, 3 * SLICE, DH), BF),
            pltpu.VMEM((MF, 2 * DH), BF),
            pltpu.VMEM((MF, 2 * DH), BF),
            pltpu.VMEM((MF, 2 * DH), F32),
            pltpu.VMEM((TOK, 2 * DH), BF),
            pltpu.VMEM((2, 4, 2, HALF, WIDTH), BF),
            pltpu.VMEM((2, 4, 2, HALF, WIDTH), BF),
            dma((6,)),
            dma((SENDS,)),
            dma((2, 4, 2)),
            dma((3, NZ)),
            dma((3, 6)),
            dma((3, 7)),
            dma((NZ,)),
            dma((NX,)),
            dma((NZ,)),
            dma((2,)),
            dma((2, 4, 2)),
        ],
        compiler_params=pltpu.CompilerParams(
            collective_id=0, has_side_effects=True, vmem_limit_bytes=60 * 1024 * 1024
        ),
    )(tokens, w_query, w_key, w_value, features, w_out.T)


def solution(mesh):
    return jax.shard_map(
        body,
        mesh=mesh,
        in_specs=(
            P("ctx", "tp"),
            P("ctx", "tp"),
            P("ctx", "tp"),
            P("ctx", "tp"),
            P("tp", None, None),
            P("tp", "ctx"),
        ),
        out_specs=P("ctx", "tp"),
        check_vma=False,
    )
```

time: 92.9 us -> 83.9 us (0.903)
  Pallas kernels: 89.1 us -> 82 us
  local copies, waits for them, and re-layouts: 3.48 us -> 1.67 us
    pallas_call x1, Pallas kernels: 89.1 us -> 82 us  [body(): pl.pallas_call(kernel, out_shape=jax.ShapeDtypeStruct((TOK, WIDTH), BF),...]
    unnamed x12 -> x1, local copies, waits for them, and re-layouts: 3.48 us -> 1.67 us
where the time goes in v2:
time: 83.9 us; the launch traced here: 83.7 us
  Pallas kernels  82 us (98%)
  local copies, waits for them, and re-layouts  1.67 us (2%)
    pallas_call x1, Pallas kernels, body(): pl.pallas_call(kernel, out_shape=jax.ShapeDtypeStruct((TOK, WIDTH), BF),...  82 us

profile of v2, /device:TPU:1, one launch (start us, length us, event | category | flops | bytes accessed | tf_op | source)
XLA Modules:
  0.0 83.7 jit_solution(1825874050019699636)
XLA Ops:
  0.0 82.0 %shard_map.64 = bf16[512,256]{1,0:T(8,128)(2,1)} custom-call(bf16[512,256]{1,0:T(8,128)(2,1)} %tok_ref.1, bf16[32,256]{1,0:T(8,128)(2,1)} %wq_ref.1, bf16[32,256]{1,0:T(8,128)(2,1)} %wk_ref.1, bf16[32,256]{1,0:T(8,128)(2,1)} %wv_ref.1, f32[2,256,128]{2,1,0:T(8,128)} %feat_ref.1, bf16[32,256]{1,0:T(8,128)(2,1)} %bitcast.1), custom_call_target="tpu_custom_call" | custom-call | tf_op jit(solution)/shard_map/pallas_call | solution.py:387
  82.0 1.7 %copy.8 = bf16[512,256]{1,0:T(8,128)(2,1)} copy(bf16[512,256]{1,0:T(8,128)(2,1)} %shard_map.64) | data formatting | bytes 524288

commit v3 on v2

--- a/solution.py
+++ b/solution.py
@@ -9,12 +9,14 @@
 GROUP = NZ * NC
 TOK = 512
 HALF = 256
+PIECES = 4
+PIECE = 128
 WIDTH = 256
 DH = 128
 MF = 256
 SHARD = 32
 SLICE = 16
-SENDS = 128
+SENDS = 192
 BF = jnp.bfloat16
 F32 = jnp.float32
 NT = (((1,), (1,)), ((), ()))
@@ -69,15 +71,6 @@
     ]
     for copy in loads:
         copy.start()
-    for copy in loads:
-        copy.wait()
-
-    for h in range(2):
-        f = feat[h]
-        hi = f.astype(BF)
-        lo = (f - hi.astype(F32)).astype(BF)
-        fcat[h] = jnp.concatenate([hi, hi, lo], axis=1)
-
     pl.semaphore_wait(barrier, len(greeted))
 
     sends = []
@@ -97,11 +90,12 @@
         return turn(y, -step if d == 0 else step, NY)
 
     def tok_part(owner, r):
-        return tok.at[owner, pl.ds(r * HALF, HALF)]
+        return tok.at[owner, pl.ds(r * PIECE, PIECE)]
 
     def tok_send(d, step, r):
         part = tok_part(tok_owner(d, step), r)
-        send(part, part, tok_sem.at[d, step, r], ups[d])
+        src = tok_ref.at[pl.ds(r * PIECE, PIECE)] if step == 0 else part
+        send(src, part, tok_sem.at[d, step, r], ups[d])
 
     def tok_recv(d, step, r):
         recv(tok_part(tok_owner(d, step + 1), r), tok_sem.at[d, step, r])
@@ -160,32 +154,42 @@
                 recv(w_part(xx, halves[d if i == 0 else 1 - d], o, part), sib_sem.at[part, 1 + 2 * d + i])
             recv(w_part(turn(x, 2, NX), halves[d], o, part), sib_sem.at[part, 5 + d])
 
-    for r in range(2):
+    for r in range(PIECES):
         for d in range(2):
             tok_send(d, 0, r)
+    for copy in loads:
+        copy.wait()
     z_send(0)
+
+    for h in range(2):
+        f = feat[h]
+        hi = f.astype(BF)
+        lo = (f - hi.astype(F32)).astype(BF)
+        fcat[h] = jnp.concatenate([hi, hi, lo], axis=1)
 
     def tok_pass(step, r):
         for d in range(2):
             tok_recv(d, step, r)
             tok_send(d, step + 1, r)
 
-    tok_pass(0, 0)
-    tok_pass(0, 1)
+    for r in range(PIECES):
+        tok_pass(0, r)
     z_recv(0)
     x_start(0)
     z_send(1)
     z_send(2)
-    tok_pass(1, 0)
-    tok_pass(1, 1)
+    for r in range(PIECES):
+        tok_pass(1, r)
     x_near(0, 0)
-    tok_recv(0, 2, 0)
-    tok_send(0, 3, 0)
+    for r in range(2):
+        tok_recv(0, 2, r)
+        tok_send(0, 3, r)
     x_near(0, 1)
     z_recv(1)
     x_start(1)
-    tok_recv(1, 2, 1)
-    tok_send(1, 3, 1)
+    for r in range(2, 4):
+        tok_recv(1, 2, r)
+        tok_send(1, 3, r)
     x_far(0)
     z_recv(2)
     sib_recv(0)
@@ -213,15 +217,17 @@
 
     x_near(1, 0)
 
-    tok_recv(0, 2, 1)
-    tok_recv(1, 2, 0)
+    for r in range(2):
+        tok_recv(0, 2, 2 + r)
+        tok_recv(1, 2, r)
 
     @pl.loop(0, 2)
     def _(i):
         kv_add(lax.rem(y + 3 + 2 * i, NY))
 
-    tok_recv(0, 3, 0)
-    tok_recv(1, 3, 1)
+    for r in range(2):
+        tok_recv(0, 3, r)
+        tok_recv(1, 3, 2 + r)
     kv_add(turn(y, 4, NY))
 
     def positive(p, h):
@@ -275,9 +281,6 @@
             @pl.when(s > 0)
             def _():
                 q[rows_r] += term
-
-    for h in range(2):
-        phiq[h] = positive(q[:, pl.ds(h * DH, DH)], h)
 
     for d in (1, 7, 2, 6, 3, 5, 4):
         zz = turn(z, d, NZ)
@@ -303,6 +306,8 @@
             nd[h, rows_r] = jnp.dot(sc, vaug[h, pl.ds(0, upto)], preferred_element_type=F32)
 
     x_near(2, 0)
+    for h in range(2):
+        phiq[h] = positive(q[:, pl.ds(h * DH, DH)], h)
     local(0)
 
     for d in range(1, NX):
@@ -341,18 +346,15 @@
     send(fsend, frecv, j_sem.at[1], sib)
     state = (before + jnp.where(c == 0, 0.0, srecv[...].astype(F32))).astype(BF)
 
-    def finish(h, state):
-        full = nd[h] + jnp.dot(phiq[h], state, preferred_element_type=F32)
+    def finish(h, state, r):
+        rows_r = pl.ds(r * HALF, HALF)
+        full = nd[h, rows_r] + jnp.dot(phiq[h, rows_r], state, preferred_element_type=F32)
         head = pl.ds(pl.multiple_of(h * DH, DH), DH)
-        attn[:, head] = (full[:, :DH] / full[:, DH:]).astype(BF)
-
-    finish(c, state)
-    recv(frecv, j_sem.at[1])
-    finish(1 - c, frecv[...])
+        attn[rows_r, head] = (full[:, :DH] / full[:, DH:]).astype(BF)
 
     def share(dest, r):
         return lax.dot_general(
-            attn[pl.ds(r * HALF, HALF)], w_rows(dest, 3), NT, preferred_element_type=F32
+            attn[pl.ds(r * PIECE, PIECE)], w_rows(dest, 3), NT, preferred_element_type=F32
         )
 
     def rs_item(d, step, r, first):
@@ -364,18 +366,25 @@
         rs_send[d, step, r] = value.astype(BF)
         send(rs_send.at[d, step, r], rs_recv.at[d, step, r], rs_sem.at[d, step, r], ups[d])
 
-    for d in range(2):
-        rs_item(d, 0, d, True)
+    finish(c, state, 0)
+    finish(c, state, 1)
+    recv(frecv, j_sem.at[1])
+    finish(1 - c, frecv[...], 0)
+    for r in range(2):
+        rs_item(0, 0, r, True)
+    finish(1 - c, frecv[...], 1)
+    for r in range(2):
+        rs_item(1, 0, 2 + r, True)
     for step in range(1, 4):
-        for k in range(2):
+        for k in range(4):
             for d in range(2):
-                rs_item(d, step, (1 - d) if k == 0 else d, step == 1 and k == 0)
-    for r in range(2):
+                rs_item(d, step, (k + 2 * (1 - d)) % 4, step == 1 and k < 2)
+    for r in range(PIECES):
         value = share(y, r)
         for d in range(2):
             recv(rs_recv.at[d, 3, r], rs_sem.at[d, 3, r])
             value = value + rs_recv[d, 3, r].astype(F32)
-        out_ref[pl.ds(r * HALF, HALF)] = value.astype(BF)
+        out_ref[pl.ds(r * PIECE, PIECE)] = value.astype(BF)
 
     for copy in sends:
         copy.wait_send()
@@ -412,11 +421,11 @@
             pltpu.VMEM((MF, 2 * DH), BF),
             pltpu.VMEM((MF, 2 * DH), F32),
             pltpu.VMEM((TOK, 2 * DH), BF),
-            pltpu.VMEM((2, 4, 2, HALF, WIDTH), BF),
-            pltpu.VMEM((2, 4, 2, HALF, WIDTH), BF),
+            pltpu.VMEM((2, 4, PIECES, PIECE, WIDTH), BF),
+            pltpu.VMEM((2, 4, PIECES, PIECE, WIDTH), BF),
             dma((6,)),
             dma((SENDS,)),
-            dma((2, 4, 2)),
+            dma((2, 4, PIECES)),
             dma((3, NZ)),
             dma((3, 6)),
             dma((3, 7)),
@@ -424,10 +433,10 @@
             dma((NX,)),
             dma((NZ,)),
             dma((2,)),
-            dma((2, 4, 2)),
+            dma((2, 4, PIECES)),
         ],
         compiler_params=pltpu.CompilerParams(
-            collective_id=0, has_side_effects=True, vmem_limit_bytes=60 * 1024 * 1024
+            collective_id=0, has_side_effects=True, vmem_limit_bytes=56 * 1024 * 1024
         ),
     )(tokens, w_query, w_key, w_value, features, w_out.T)
 

time: 83.9 us -> 83.4 us (level)
  no operation moved by 1% of the time
where the time goes in v3:
time: 83.4 us; the launch traced here: 83.2 us
  Pallas kernels  81.5 us (98%)
  local copies, waits for them, and re-layouts  1.67 us (2%)
    pallas_call x1, Pallas kernels, body(): pl.pallas_call(kernel, out_shape=jax.ShapeDtypeStruct((TOK, WIDTH), BF),...  81.5 us
    unnamed x1, local copies, waits for them, and re-layouts  1.67 us

profile of v3, /device:TPU:1, one launch (start us, length us, event | category | flops | bytes accessed | tf_op | source)
XLA Modules:
  0.0 83.2 jit_solution(12136522870003507462)
XLA Ops:
  0.0 81.5 %shard_map.64 = bf16[512,256]{1,0:T(8,128)(2,1)} custom-call(bf16[512,256]{1,0:T(8,128)(2,1)} %tok_ref.1, bf16[32,256]{1,0:T(8,128)(2,1)} %wq_ref.1, bf16[32,256]{1,0:T(8,128)(2,1)} %wk_ref.1, bf16[32,256]{1,0:T(8,128)(2,1)} %wv_ref.1, f32[2,256,128]{2,1,0:T(8,128)} %feat_ref.1, bf16[32,256]{1,0:T(8,128)(2,1)} %bitcast.1), custom_call_target="tpu_custom_call" | custom-call | tf_op jit(solution)/shard_map/pallas_call | solution.py:396
  81.6 1.7 %copy.8 = bf16[512,256]{1,0:T(8,128)(2,1)} copy(bf16[512,256]{1,0:T(8,128)(2,1)} %shard_map.64) | data formatting | bytes 524288

commit v4 on v3

--- a/solution.py
+++ b/solution.py
@@ -16,6 +16,7 @@
 MF = 256
 SHARD = 32
 SLICE = 16
+SROWS = DH + SLICE
 SENDS = 192
 BF = jnp.bfloat16
 F32 = jnp.float32
@@ -25,9 +26,9 @@
 
 def kernel(
     tok_ref, wq_ref, wk_ref, wv_ref, feat_ref, wo_ref, out_ref,
-    tok, w, kv, q, vaug, phik, phiq, feat, fcat, nd, ssend, srecv, tsend, arecv, excl, tot,
-    psend, pfx, fsend, frecv, own, attn, rs_send, rs_recv,
-    loc_sem, ssem, tok_sem, z_sem, x_sem, sib_sem, a_sem, b_sem, c_sem, j_sem, rs_sem,
+    tok, w, kv, q, vaug, phik, phiq, feat, fcat, nd, sacc, ssend, srecv, tsend, arecv, nsend, nrecv,
+    excl, tot, ntot, psend, pfx, npre, fsend, frecv, own, attn, rs_send, rs_recv,
+    loc_sem, ssem, tok_sem, z_sem, x_sem, sib_sem, a_sem, an_sem, b_sem, bn_sem, c_sem, j_sem, rs_sem,
 ):
     ctx = lax.axis_index("ctx")
     y = lax.axis_index("tp")
@@ -166,6 +167,7 @@
         hi = f.astype(BF)
         lo = (f - hi.astype(F32)).astype(BF)
         fcat[h] = jnp.concatenate([hi, hi, lo], axis=1)
+        vaug[h, :, pl.ds(DH, DH)] = jnp.ones((TOK, DH), BF)
 
     def tok_pass(step, r):
         for d in range(2):
@@ -225,11 +227,6 @@
     def _(i):
         kv_add(lax.rem(y + 3 + 2 * i, NY))
 
-    for r in range(2):
-        tok_recv(0, 3, r)
-        tok_recv(1, 3, 2 + r)
-    kv_add(turn(y, 4, NY))
-
     def positive(p, h):
         s = p * (DH ** -0.25)
         half_square = 0.5 * jnp.sum(s * s, axis=-1, keepdims=True)
@@ -240,27 +237,51 @@
         )
         return jnp.exp(logits - half_square).astype(BF)
 
-    def key_sums(h):
-        head = pl.ds(pl.multiple_of(h * DH, DH), DH)
-        vaug[h, :, pl.ds(0, DH)] = kv[1, :, head].astype(BF)
-        vaug[h, :, pl.ds(DH, DH)] = jnp.ones((TOK, DH), BF)
-        phik[h] = positive(kv[0, :, head], h)
-        return lax.dot_general(phik[h], vaug[h], TN, preferred_element_type=F32)
-
-    ssend[...] = key_sums(1 - c).astype(BF)
+    last = turn(y, 4, NY)
+
+    def key_rows(r):
+        rows_r = pl.ds(r * PIECE, PIECE)
+        t = tok[last, rows_r]
+        k = kv[0, rows_r] + jnp.dot(t, w_rows(last, 0), preferred_element_type=F32)
+        v = kv[1, rows_r] + jnp.dot(t, w_rows(last, 1), preferred_element_type=F32)
+        for h in range(2):
+            phik[h, rows_r] = positive(k[:, h * DH : (h + 1) * DH], h)
+            vaug[h, rows_r, pl.ds(0, DH)] = v[:, h * DH : (h + 1) * DH].astype(BF)
+
+    def key_pair(p):
+        tok_recv(0, 3, p)
+        tok_recv(1, 3, 2 + p)
+        key_rows(p)
+        key_rows(2 + p)
+
+    def key_sums(h, p):
+        spans_p = [pl.ds(r * PIECE, PIECE) for r in (p, 2 + p)]
+        return lax.dot_general(
+            jnp.concatenate([vaug[h, rows_r] for rows_r in spans_p], axis=0),
+            jnp.concatenate([phik[h, rows_r] for rows_r in spans_p], axis=0),
+            TN, preferred_element_type=F32,
+        )[:SROWS]
+
+    key_pair(0)
+    for h in range(2):
+        sacc[h] = key_sums(h, 0)
+    key_pair(1)
+    ssend[...] = (sacc[1 - c] + key_sums(1 - c, 1)).astype(BF)
     send(ssend, srecv, j_sem.at[0], sib)
-    own[...] = key_sums(c).astype(BF).astype(F32)
+    own[...] = (sacc[c] + key_sums(c, 1)).astype(BF).astype(F32)
     recv(srecv, j_sem.at[0])
-    chip = own[...] + srecv[...].astype(F32)
-    lane = lax.broadcasted_iota(jnp.int32, (NZ, SLICE, DH), 2)
-    norm = chip[:, DH:].reshape(NZ, 2, SLICE, DH)
-    tsend[:, pl.ds(0, 2 * SLICE)] = chip[:, :DH].reshape(NZ, 2 * SLICE, DH).astype(BF)
-    tsend[:, pl.ds(2 * SLICE, SLICE)] = jnp.where(lane < DH // 2, norm[:, 0], norm[:, 1]).astype(BF)
+    chip = (own[...] + srecv[...].astype(F32)).astype(BF)
+    tsend[...] = chip[:DH].reshape(NZ, SLICE, MF)
+    nsend[...] = chip[DH:]
 
     for d in (4, 3, 5, 2, 6, 1, 7):
         zz = turn(z, d, NZ)
         send(tsend.at[zz], arecv.at[z], a_sem.at[z], at(x, zz, c))
+    for d in (4, 3, 5, 2, 6, 1, 7):
+        zz = turn(z, d, NZ)
+        send(nsend, nrecv.at[z], an_sem.at[z], at(x, zz, c))
     arecv[z] = tsend[z]
+    nrecv[z] = nsend[...]
 
     x_near(1, 1)
     x_start(2)
@@ -285,13 +306,23 @@
     for d in (1, 7, 2, 6, 3, 5, 4):
         zz = turn(z, d, NZ)
         recv(arecv.at[zz], a_sem.at[zz])
-    run = jnp.zeros((3 * SLICE, DH), F32)
+    run = jnp.zeros((SLICE, MF), F32)
     for i in range(NZ):
         excl[i] = run
         run = run + arecv[i].astype(F32)
     tot[x] = run.astype(BF)
     for d in (2, 1, 3):
         send(tot.at[x], tot.at[x], b_sem.at[x], at(turn(x, d, NX), z, c))
+
+    for d in (1, 7, 2, 6, 3, 5, 4):
+        zz = turn(z, d, NZ)
+        recv(nrecv.at[zz], an_sem.at[zz])
+    run = jnp.zeros((SLICE, MF), F32)
+    for i in range(NZ):
+        run = run + nrecv[i].astype(F32)
+    ntot[x] = run.astype(BF)
+    for d in (2, 1, 3):
+        send(ntot.at[x], ntot.at[x], bn_sem.at[x], at(turn(x, d, NX), z, c))
 
     def local(h):
         for r in range(2):
@@ -313,7 +344,7 @@
     for d in range(1, NX):
         xx = turn(x, d, NX)
         recv(tot.at[xx], b_sem.at[xx])
-    base = jnp.zeros((3 * SLICE, DH), F32)
+    base = jnp.zeros((SLICE, MF), F32)
     for i in range(NX):
         base = base + jnp.where(i < x, tot[i].astype(F32), 0.0)
     for i in range(NZ):
@@ -328,27 +359,33 @@
     x_far(2)
     sib_recv(2)
 
+    for d in range(1, NX):
+        xx = turn(x, d, NX)
+        recv(ntot.at[xx], bn_sem.at[xx])
+    base = jnp.zeros((SLICE, MF), F32)
+    for i in range(NX):
+        base = base + jnp.where(i < x, ntot[i].astype(F32), 0.0)
+    for i in range(NZ):
+        base = base + jnp.where(i < z, nrecv[i].astype(F32), 0.0)
+    npre[...] = base
+
     for d in (1, 7, 2, 6, 3, 5, 4):
         zz = turn(z, d, NZ)
         recv(pfx.at[zz], c_sem.at[zz])
 
-    pick_r = lax.broadcasted_iota(jnp.int32, (DH, 2 * DH), 0)
-    pick_c = lax.broadcasted_iota(jnp.int32, (DH, 2 * DH), 1)
-    pick = (pick_r == jnp.where(pick_c < DH, 0, DH // 2)).astype(F32).astype(BF)
-    spread = jnp.dot(
-        pfx[:, pl.ds(2 * SLICE, SLICE)].reshape(NZ * SLICE, DH), pick, preferred_element_type=F32
-    ).reshape(NZ, SLICE, 2 * DH)
-    norm = jnp.stack([spread[:, :, :DH], spread[:, :, DH:]], axis=1).reshape(MF, DH)
-    before = jnp.concatenate(
-        [pfx[:, pl.ds(0, 2 * SLICE)].reshape(MF, DH).astype(F32), norm], axis=1
-    )
+    before = jnp.concatenate([pfx[...].reshape(DH, MF).astype(F32), npre[...]], axis=0)
     fsend[...] = (before + jnp.where(c == 0, own[...], 0.0)).astype(BF)
     send(fsend, frecv, j_sem.at[1], sib)
     state = (before + jnp.where(c == 0, 0.0, srecv[...].astype(F32))).astype(BF)
 
+    def spread(sums):
+        return jnp.concatenate([sums[:DH]] + [sums[DH:]] * (DH // SLICE), axis=0)
+
     def finish(h, state, r):
         rows_r = pl.ds(r * HALF, HALF)
-        full = nd[h, rows_r] + jnp.dot(phiq[h, rows_r], state, preferred_element_type=F32)
+        full = nd[h, rows_r] + lax.dot_general(
+            phiq[h, rows_r], state, NT, preferred_element_type=F32
+        )
         head = pl.ds(pl.multiple_of(h * DH, DH), DH)
         attn[rows_r, head] = (full[:, :DH] / full[:, DH:]).astype(BF)
 
@@ -366,13 +403,15 @@
         rs_send[d, step, r] = value.astype(BF)
         send(rs_send.at[d, step, r], rs_recv.at[d, step, r], rs_sem.at[d, step, r], ups[d])
 
+    state = spread(state)
     finish(c, state, 0)
     finish(c, state, 1)
     recv(frecv, j_sem.at[1])
-    finish(1 - c, frecv[...], 0)
+    state = spread(frecv[...])
+    finish(1 - c, state, 0)
     for r in range(2):
         rs_item(0, 0, r, True)
-    finish(1 - c, frecv[...], 1)
+    finish(1 - c, state, 1)
     for r in range(2):
         rs_item(1, 0, 2 + r, True)
     for step in range(1, 4):
@@ -409,17 +448,22 @@
             pltpu.VMEM((2, MF, DH), F32),
             pltpu.VMEM((2, MF, 3 * DH), BF),
             pltpu.VMEM((2, TOK, 2 * DH), F32),
-            pltpu.VMEM((MF, 2 * DH), BF),
-            pltpu.VMEM((MF, 2 * DH), BF),
-            pltpu.VMEM((NZ, 3 * SLICE, DH), BF),
-            pltpu.VMEM((NZ, 3 * SLICE, DH), BF),
-            pltpu.VMEM((NZ, 3 * SLICE, DH), F32),
-            pltpu.VMEM((NX, 3 * SLICE, DH), BF),
-            pltpu.VMEM((NZ, 3 * SLICE, DH), BF),
-            pltpu.VMEM((NZ, 3 * SLICE, DH), BF),
-            pltpu.VMEM((MF, 2 * DH), BF),
-            pltpu.VMEM((MF, 2 * DH), BF),
-            pltpu.VMEM((MF, 2 * DH), F32),
+            pltpu.VMEM((2, SROWS, MF), F32),
+            pltpu.VMEM((SROWS, MF), BF),
+            pltpu.VMEM((SROWS, MF), BF),
+            pltpu.VMEM((NZ, SLICE, MF), BF),
+            pltpu.VMEM((NZ, SLICE, MF), BF),
+            pltpu.VMEM((SLICE, MF), BF),
+            pltpu.VMEM((NZ, SLICE, MF), BF),
+            pltpu.VMEM((NZ, SLICE, MF), F32),
+            pltpu.VMEM((NX, SLICE, MF), BF),
+            pltpu.VMEM((NX, SLICE, MF), BF),
+            pltpu.VMEM((NZ, SLICE, MF), BF),
+            pltpu.VMEM((NZ, SLICE, MF), BF),
+            pltpu.VMEM((SLICE, MF), F32),
+            pltpu.VMEM((SROWS, MF), BF),
+            pltpu.VMEM((SROWS, MF), BF),
+            pltpu.VMEM((SROWS, MF), F32),
             pltpu.VMEM((TOK, 2 * DH), BF),
             pltpu.VMEM((2, 4, PIECES, PIECE, WIDTH), BF),
             pltpu.VMEM((2, 4, PIECES, PIECE, WIDTH), BF),
@@ -430,6 +474,8 @@
             dma((3, 6)),
             dma((3, 7)),
             dma((NZ,)),
+            dma((NZ,)),
+            dma((NX,)),
             dma((NX,)),
             dma((NZ,)),
             dma((2,)),

time: 83.4 us -> 83.6 us (level)
  no operation moved by 1% of the time
where the time goes in v4:
time: 83.6 us; the launch traced here: 83.5 us
  Pallas kernels  81.8 us (98%)
  local copies, waits for them, and re-layouts  1.67 us (2%)
    pallas_call x1, Pallas kernels, body(): pl.pallas_call(kernel, out_shape=jax.ShapeDtypeStruct((TOK, WIDTH), BF),...  81.8 us

profile of v4, /device:TPU:1, one launch (start us, length us, event | category | flops | bytes accessed | tf_op | source)
XLA Modules:
  0.0 83.5 jit_solution(5195208667261483916)
XLA Ops:
  0.0 81.8 %shard_map.64 = bf16[512,256]{1,0:T(8,128)(2,1)} custom-call(bf16[512,256]{1,0:T(8,128)(2,1)} %tok_ref.1, bf16[32,256]{1,0:T(8,128)(2,1)} %wq_ref.1, bf16[32,256]{1,0:T(8,128)(2,1)} %wk_ref.1, bf16[32,256]{1,0:T(8,128)(2,1)} %wv_ref.1, f32[2,256,128]{2,1,0:T(8,128)} %feat_ref.1, bf16[32,256]{1,0:T(8,128)(2,1)} %bitcast.1), custom_call_target="tpu_custom_call" | custom-call | tf_op jit(solution)/shard_map/pallas_call | solution.py:435
  81.8 1.7 %copy.8 = bf16[512,256]{1,0:T(8,128)(2,1)} copy(bf16[512,256]{1,0:T(8,128)(2,1)} %shard_map.64) | data formatting | bytes 524288

commit v5 on v4

--- a/solution.py
+++ b/solution.py
@@ -17,7 +17,7 @@
 SHARD = 32
 SLICE = 16
 SROWS = DH + SLICE
-SENDS = 192
+SENDS = 256
 BF = jnp.bfloat16
 F32 = jnp.float32
 NT = (((1,), (1,)), ((), ()))
@@ -28,7 +28,7 @@
     tok_ref, wq_ref, wk_ref, wv_ref, feat_ref, wo_ref, out_ref,
     tok, w, kv, q, vaug, phik, phiq, feat, fcat, nd, sacc, ssend, srecv, tsend, arecv, nsend, nrecv,
     excl, tot, ntot, psend, pfx, npre, fsend, frecv, own, attn, rs_send, rs_recv,
-    loc_sem, ssem, tok_sem, z_sem, x_sem, sib_sem, a_sem, an_sem, b_sem, bn_sem, c_sem, j_sem, rs_sem,
+    loc_sem, ssem, tok_sem, z_sem, n_sem, f_sem, k_sem, x_sem, sib_sem, a_sem, an_sem, b_sem, bn_sem, c_sem, j_sem, rs_sem,
 ):
     ctx = lax.axis_index("ctx")
     y = lax.axis_index("tp")
@@ -108,7 +108,7 @@
 
     def z_send(part):
         mine = w_part(x, z, c, part)
-        for d in (4, 3, 5, 2, 6, 1, 7):
+        for d in (1, 7, 2, 6, 3, 5, 4):
             send(mine, mine, z_sem.at[part, z], at(x, turn(z, d, NZ), c))
 
     def z_recv(part):
@@ -155,12 +155,48 @@
                 recv(w_part(xx, halves[d if i == 0 else 1 - d], o, part), sib_sem.at[part, 1 + 2 * d + i])
             recv(w_part(turn(x, 2, NX), halves[d], o, part), sib_sem.at[part, 5 + d])
 
+    def one(xx, off, cc):
+        return w_part(xx, turn(z, off, NZ), cc, 0)
+
+    def near_send(offs):
+        for o in offs:
+            shard = one(x, o, c)
+            for d in range(2):
+                send(shard, shard, n_sem.at[d, o], sides[d])
+            send(shard, shard, k_sem.at[0, o], sib)
+
+    def z_group(offs):
+        for o in offs:
+            recv(one(x, o, c), z_sem.at[0, turn(z, o, NZ)])
+        near_send(offs)
+
+    def near_group(offs):
+        for o in offs:
+            for d in range(2):
+                shard = one(turn(x, -1 if d == 0 else 1, NX), o, c)
+                recv(shard, n_sem.at[d, o])
+                if (o < NZ // 2) == (d == 0):
+                    send(shard, shard, f_sem.at[o], sides[d])
+                send(shard, shard, k_sem.at[1 + d, o], sib)
+
+    def far_group(offs):
+        for o in offs:
+            shard = one(turn(x, 2, NX), o, c)
+            recv(shard, f_sem.at[o])
+            send(shard, shard, k_sem.at[3, o], sib)
+
+    def key_weights():
+        for i, by in enumerate((0, -1, 1, 2)):
+            for o in range(NZ):
+                recv(one(turn(x, by, NX), o, 1 - c), k_sem.at[i, o])
+
     for r in range(PIECES):
         for d in range(2):
             tok_send(d, 0, r)
     for copy in loads:
         copy.wait()
     z_send(0)
+    near_send((0,))
 
     for h in range(2):
         f = feat[h]
@@ -174,58 +210,60 @@
             tok_recv(d, step, r)
             tok_send(d, step + 1, r)
 
-    for r in range(PIECES):
-        tok_pass(0, r)
-    z_recv(0)
-    x_start(0)
+    groups = ((0,), (1, 7), (2, 6), (3, 5, 4))
+    tok_pass(0, 0)
+    z_group(groups[1])
+    tok_pass(0, 1)
+    z_group(groups[2])
+    near_group(groups[0])
+    tok_pass(0, 2)
+    z_group(groups[3])
+    near_group(groups[1])
     z_send(1)
     z_send(2)
-    for r in range(PIECES):
-        tok_pass(1, r)
-    x_near(0, 0)
+    tok_pass(0, 3)
+    near_group(groups[2])
+    tok_pass(1, 0)
+    near_group(groups[3])
+    far_group(groups[0])
+    tok_pass(1, 1)
+    far_group(groups[1])
+    tok_pass(1, 2)
+    far_group(groups[2])
+    tok_pass(1, 3)
+    far_group(groups[3])
+    z_recv(1)
+    x_start(1)
     for r in range(2):
         tok_recv(0, 2, r)
         tok_send(0, 3, r)
-    x_near(0, 1)
-    z_recv(1)
-    x_start(1)
+    key_weights()
     for r in range(2, 4):
         tok_recv(1, 2, r)
         tok_send(1, 3, r)
-    x_far(0)
     z_recv(2)
-    sib_recv(0)
 
     def w_rows(s, k):
         return w[lax.div(s, 2), pl.ds(lax.rem(s, 2) * 4, 4), :, k].reshape(WIDTH, WIDTH)
 
-    def kv_term(s, r):
-        t = tok[s, pl.ds(r * HALF, HALF)]
-        k = jnp.dot(t, w_rows(s, 0), preferred_element_type=F32)
-        v = jnp.dot(t, w_rows(s, 1), preferred_element_type=F32)
-        return k, v
-
-    def kv_add(s):
-        for r in range(2):
-            k, v = kv_term(s, r)
-            kv[0, pl.ds(r * HALF, HALF)] += k
-            kv[1, pl.ds(r * HALF, HALF)] += v
-
-    kv[...] = jnp.zeros_like(kv)
-
-    @pl.loop(0, 5)
-    def _(i):
-        kv_add(lax.rem(y + i + (NY - 2), NY))
-
+    def early(by, add):
+        shards = [turn(y, d, NY) for d in by]
+
+        @pl.loop(0, 2)
+        def _(r):
+            rows_r = pl.ds(pl.multiple_of(r * HALF, HALF), HALF)
+            t = jnp.concatenate([tok[s, rows_r] for s in shards], axis=1)
+            for k in range(2):
+                wide = jnp.concatenate([w_rows(s, k) for s in shards], axis=0)
+                value = jnp.dot(t, wide, preferred_element_type=F32)
+                kv[k, rows_r] = kv[k, rows_r] + value if add else value
+
+    early((0, 1, -1, 2, -2), False)
     x_near(1, 0)
-
     for r in range(2):
         tok_recv(0, 2, 2 + r)
         tok_recv(1, 2, r)
-
-    @pl.loop(0, 2)
-    def _(i):
-        kv_add(lax.rem(y + 3 + 2 * i, NY))
+    early((3, -3), True)
 
     def positive(p, h):
         s = p * (DH ** -0.25)
@@ -288,20 +326,13 @@
     x_far(1)
     sib_recv(1)
 
-    @pl.loop(0, NY)
-    def _(s):
-        for r in range(2):
-            t = tok[s, pl.ds(r * HALF, HALF)]
-            term = jnp.dot(t, w_rows(s, 2), preferred_element_type=F32)
-            rows_r = pl.ds(r * HALF, HALF)
-
-            @pl.when(s == 0)
-            def _():
-                q[rows_r] = term
-
-            @pl.when(s > 0)
-            def _():
-                q[rows_r] += term
+    @pl.loop(0, 2)
+    def _(r):
+        rows_r = pl.ds(pl.multiple_of(r * HALF, HALF), HALF)
+        t = jnp.concatenate([tok[s, rows_r] for s in range(NY)], axis=1)
+        q[rows_r] = jnp.dot(
+            t, w[:, :, :, 2].reshape(NY * WIDTH, WIDTH), preferred_element_type=F32
+        )
 
     for d in (1, 7, 2, 6, 3, 5, 4):
         zz = turn(z, d, NZ)
@@ -471,6 +502,9 @@
             dma((SENDS,)),
             dma((2, 4, PIECES)),
             dma((3, NZ)),
+            dma((2, NZ)),
+            dma((NZ,)),
+            dma((4, NZ)),
             dma((3, 6)),
             dma((3, 7)),
             dma((NZ,)),

time: 83.6 us -> 83.5 us (level)
  no operation moved by 1% of the time
where the time goes in v5:
time: 83.5 us; the launch traced here: 83.4 us
  Pallas kernels  81.7 us (98%)
  local copies, waits for them, and re-layouts  1.67 us (2%)
    pallas_call x1, Pallas kernels, body(): pl.pallas_call(kernel, out_shape=jax.ShapeDtypeStruct((TOK, WIDTH), BF),...  81.7 us
    unnamed x1, local copies, waits for them, and re-layouts  1.67 us

profile of v5, /device:TPU:1, one launch (start us, length us, event | category | flops | bytes accessed | tf_op | source)
XLA Modules:
  0.0 83.4 jit_solution(3714505544042461466)
XLA Ops:
  0.0 81.7 %shard_map.64 = bf16[512,256]{1,0:T(8,128)(2,1)} custom-call(bf16[512,256]{1,0:T(8,128)(2,1)} %tok_ref.1, bf16[32,256]{1,0:T(8,128)(2,1)} %wq_ref.1, bf16[32,256]{1,0:T(8,128)(2,1)} %wk_ref.1, bf16[32,256]{1,0:T(8,128)(2,1)} %wv_ref.1, f32[2,256,128]{2,1,0:T(8,128)} %feat_ref.1, bf16[32,256]{1,0:T(8,128)(2,1)} %bitcast.1), custom_call_target="tpu_custom_call" | custom-call | tf_op jit(solution)/shard_map/pallas_call | solution.py:466
  81.7 1.7 %copy.8 = bf16[512,256]{1,0:T(8,128)(2,1)} copy(bf16[512,256]{1,0:T(8,128)(2,1)} %shard_map.64) | data formatting | bytes 524288

commit v6 on v4

--- a/solution.py
+++ b/solution.py
@@ -27,7 +27,7 @@
 def kernel(
     tok_ref, wq_ref, wk_ref, wv_ref, feat_ref, wo_ref, out_ref,
     tok, w, kv, q, vaug, phik, phiq, feat, fcat, nd, sacc, ssend, srecv, tsend, arecv, nsend, nrecv,
-    excl, tot, ntot, psend, pfx, npre, fsend, frecv, own, attn, rs_send, rs_recv,
+    excl, tot, ntot, psend, pfx, npre, fsend, frecv, own, attn, rs_send, rs_recv, result,
     loc_sem, ssem, tok_sem, z_sem, x_sem, sib_sem, a_sem, an_sem, b_sem, bn_sem, c_sem, j_sem, rs_sem,
 ):
     ctx = lax.axis_index("ctx")
@@ -199,33 +199,21 @@
     def w_rows(s, k):
         return w[lax.div(s, 2), pl.ds(lax.rem(s, 2) * 4, 4), :, k].reshape(WIDTH, WIDTH)
 
-    def kv_term(s, r):
-        t = tok[s, pl.ds(r * HALF, HALF)]
-        k = jnp.dot(t, w_rows(s, 0), preferred_element_type=F32)
-        v = jnp.dot(t, w_rows(s, 1), preferred_element_type=F32)
-        return k, v
-
-    def kv_add(s):
-        for r in range(2):
-            k, v = kv_term(s, r)
-            kv[0, pl.ds(r * HALF, HALF)] += k
-            kv[1, pl.ds(r * HALF, HALF)] += v
-
-    kv[...] = jnp.zeros_like(kv)
-
-    @pl.loop(0, 5)
-    def _(i):
-        kv_add(lax.rem(y + i + (NY - 2), NY))
-
-    x_near(1, 0)
-
     for r in range(2):
         tok_recv(0, 2, 2 + r)
         tok_recv(1, 2, r)
 
+    early = [turn(y, d, NY) for d in (0, 1, -1, 2, -2, 3, -3)]
+
     @pl.loop(0, 2)
-    def _(i):
-        kv_add(lax.rem(y + 3 + 2 * i, NY))
+    def _(r):
+        rows_r = pl.ds(pl.multiple_of(r * HALF, HALF), HALF)
+        t = jnp.concatenate([tok[s, rows_r] for s in early], axis=1)
+        for k in range(2):
+            wide = jnp.concatenate([w_rows(s, k) for s in early], axis=0)
+            kv[k, rows_r] = jnp.dot(t, wide, preferred_element_type=F32)
+
+    x_near(1, 0)
 
     def positive(p, h):
         s = p * (DH ** -0.25)
@@ -288,20 +276,13 @@
     x_far(1)
     sib_recv(1)
 
-    @pl.loop(0, NY)
-    def _(s):
-        for r in range(2):
-            t = tok[s, pl.ds(r * HALF, HALF)]
-            term = jnp.dot(t, w_rows(s, 2), preferred_element_type=F32)
-            rows_r = pl.ds(r * HALF, HALF)
-
-            @pl.when(s == 0)
-            def _():
-                q[rows_r] = term
-
-            @pl.when(s > 0)
-            def _():
-                q[rows_r] += term
+    @pl.loop(0, 2)
+    def _(r):
+        rows_r = pl.ds(pl.multiple_of(r * HALF, HALF), HALF)
+        t = jnp.concatenate([tok[s, rows_r] for s in range(NY)], axis=1)
+        q[rows_r] = jnp.dot(
+            t, w[:, :, :, 2].reshape(NY * WIDTH, WIDTH), preferred_element_type=F32
+        )
 
     for d in (1, 7, 2, 6, 3, 5, 4):
         zz = turn(z, d, NZ)
@@ -402,6 +383,14 @@
             value = value + rs_recv[d, step - 1, r].astype(F32)
         rs_send[d, step, r] = value.astype(BF)
         send(rs_send.at[d, step, r], rs_recv.at[d, step, r], rs_sem.at[d, step, r], ups[d])
+
+    before_ring = len(sends)
+    waited = []
+
+    def drain(count, stop):
+        for copy in sends[len(waited) : min(len(waited) + count, stop)]:
+            copy.wait_send()
+            waited.append(copy)
 
     state = spread(state)
     finish(c, state, 0)
@@ -418,15 +407,23 @@
         for k in range(4):
             for d in range(2):
                 rs_item(d, step, (k + 2 * (1 - d)) % 4, step == 1 and k < 2)
+                drain(before_ring // 20, before_ring)
+    drain(len(sends), len(sends) - 8)
+    stores = []
     for r in range(PIECES):
         value = share(y, r)
         for d in range(2):
             recv(rs_recv.at[d, 3, r], rs_sem.at[d, 3, r])
             value = value + rs_recv[d, 3, r].astype(F32)
-        out_ref[pl.ds(r * PIECE, PIECE)] = value.astype(BF)
-
-    for copy in sends:
-        copy.wait_send()
+        rows_r = pl.ds(r * PIECE, PIECE)
+        result[rows_r] = value.astype(BF)
+        store = pltpu.make_async_copy(result.at[rows_r], out_ref.at[rows_r], loc_sem.at[r])
+        store.start()
+        stores.append(store)
+
+    drain(len(sends), len(sends))
+    for store in stores:
+        store.wait()
 
 
 def body(tokens, w_query, w_key, w_value, features, w_out):
@@ -436,7 +433,7 @@
         kernel,
         out_shape=jax.ShapeDtypeStruct((TOK, WIDTH), BF),
         in_specs=[hbm] * 6,
-        out_specs=pl.BlockSpec(memory_space=pltpu.VMEM),
+        out_specs=hbm,
         scratch_shapes=[
             pltpu.VMEM((NY, TOK, WIDTH), BF),
             pltpu.VMEM((NX, NZ, NC, 4, SHARD, WIDTH), BF),
@@ -467,6 +464,7 @@
             pltpu.VMEM((TOK, 2 * DH), BF),
             pltpu.VMEM((2, 4, PIECES, PIECE, WIDTH), BF),
             pltpu.VMEM((2, 4, PIECES, PIECE, WIDTH), BF),
+            pltpu.VMEM((TOK, WIDTH), BF),
             dma((6,)),
             dma((SENDS,)),
             dma((2, 4, PIECES)),

time: 83.6 us -> 82.3 us (0.984)
  Pallas kernels: 81.8 us -> 80.4 us
    pallas_call x1, Pallas kernels: 81.8 us -> 80.4 us  [body(): pl.pallas_call(kernel, out_shape=jax.ShapeDtypeStruct((TOK, WIDTH), BF),...]
where the time goes in v6:
time: 82.3 us; the launch traced here: 82.1 us
  Pallas kernels  80.4 us (98%)
  local copies, waits for them, and re-layouts  1.67 us (2%)
    pallas_call x1, Pallas kernels, body(): pl.pallas_call(kernel, out_shape=jax.ShapeDtypeStruct((TOK, WIDTH), BF),...  80.4 us
    unnamed x1, local copies, waits for them, and re-layouts  1.67 us

profile of v6, /device:TPU:1, one launch (start us, length us, event | category | flops | bytes accessed | tf_op | source)
XLA Modules:
  0.0 82.1 jit_solution(15466152565346822342)
XLA Ops:
  0.0 80.4 %shard_map.64 = bf16[512,256]{1,0:T(8,128)(2,1)} custom-call(bf16[512,256]{1,0:T(8,128)(2,1)} %tok_ref.1, bf16[32,256]{1,0:T(8,128)(2,1)} %wq_ref.1, bf16[32,256]{1,0:T(8,128)(2,1)} %wk_ref.1, bf16[32,256]{1,0:T(8,128)(2,1)} %wv_ref.1, f32[2,256,128]{2,1,0:T(8,128)} %feat_ref.1, bf16[32,256]{1,0:T(8,128)(2,1)} %bitcast.1), custom_call_target="tpu_custom_call" | custom-call | tf_op jit(solution)/shard_map/pallas_call | solution.py:432
  80.5 1.7 %copy.8 = bf16[512,256]{1,0:T(8,128)(2,1)} copy(bf16[512,256]{1,0:T(8,128)(2,1)} %shard_map.64) | data formatting | bytes 524288

commit v7 on v6

--- a/solution.py
+++ b/solution.py
@@ -213,7 +213,6 @@
             wide = jnp.concatenate([w_rows(s, k) for s in early], axis=0)
             kv[k, rows_r] = jnp.dot(t, wide, preferred_element_type=F32)
 
-    x_near(1, 0)
 
     def positive(p, h):
         s = p * (DH ** -0.25)
@@ -227,20 +226,22 @@
 
     last = turn(y, 4, NY)
 
-    def key_rows(r):
-        rows_r = pl.ds(r * PIECE, PIECE)
-        t = tok[last, rows_r]
-        k = kv[0, rows_r] + jnp.dot(t, w_rows(last, 0), preferred_element_type=F32)
-        v = kv[1, rows_r] + jnp.dot(t, w_rows(last, 1), preferred_element_type=F32)
-        for h in range(2):
-            phik[h, rows_r] = positive(k[:, h * DH : (h + 1) * DH], h)
-            vaug[h, rows_r, pl.ds(0, DH)] = v[:, h * DH : (h + 1) * DH].astype(BF)
-
     def key_pair(p):
         tok_recv(0, 3, p)
         tok_recv(1, 3, 2 + p)
-        key_rows(p)
-        key_rows(2 + p)
+        rows_p = [pl.ds(r * PIECE, PIECE) for r in (p, 2 + p)]
+        t = jnp.concatenate([tok[last, rows_r] for rows_r in rows_p], axis=0)
+        both = []
+        for k in range(2):
+            had = jnp.concatenate([kv[k, rows_r] for rows_r in rows_p], axis=0)
+            both.append(had + jnp.dot(t, w_rows(last, k), preferred_element_type=F32))
+        for h in range(2):
+            head = slice(h * DH, (h + 1) * DH)
+            maps = positive(both[0][:, head], h)
+            vals = both[1][:, head].astype(BF)
+            for i, rows_r in enumerate(rows_p):
+                phik[h, rows_r] = maps[i * PIECE : (i + 1) * PIECE]
+                vaug[h, rows_r, pl.ds(0, DH)] = vals[i * PIECE : (i + 1) * PIECE]
 
     def key_sums(h, p):
         spans_p = [pl.ds(r * PIECE, PIECE) for r in (p, 2 + p)]
@@ -256,6 +257,7 @@
     key_pair(1)
     ssend[...] = (sacc[1 - c] + key_sums(1 - c, 1)).astype(BF)
     send(ssend, srecv, j_sem.at[0], sib)
+    x_near(1, 0)
     own[...] = (sacc[c] + key_sums(c, 1)).astype(BF).astype(F32)
     recv(srecv, j_sem.at[0])
     chip = (own[...] + srecv[...].astype(F32)).astype(BF)

time: 82.3 us -> 81.9 us (level)
  no operation moved by 1% of the time
where the time goes in v7:
time: 81.9 us; the launch traced here: 81.8 us
  Pallas kernels  80.1 us (98%)
  local copies, waits for them, and re-layouts  1.67 us (2%)
    pallas_call x1, Pallas kernels, body(): pl.pallas_call(kernel, out_shape=jax.ShapeDtypeStruct((TOK, WIDTH), BF),...  80.1 us
    unnamed x1, local copies, waits for them, and re-layouts  1.67 us

profile of v7, /device:TPU:1, one launch (start us, length us, event | category | flops | bytes accessed | tf_op | source)
XLA Modules:
  0.0 81.8 jit_solution(6166403258489464714)
XLA Ops:
  0.0 80.1 %shard_map.64 = bf16[512,256]{1,0:T(8,128)(2,1)} custom-call(bf16[512,256]{1,0:T(8,128)(2,1)} %tok_ref.1, bf16[32,256]{1,0:T(8,128)(2,1)} %wq_ref.1, bf16[32,256]{1,0:T(8,128)(2,1)} %wk_ref.1, bf16[32,256]{1,0:T(8,128)(2,1)} %wv_ref.1, f32[2,256,128]{2,1,0:T(8,128)} %feat_ref.1, bf16[32,256]{1,0:T(8,128)(2,1)} %bitcast.1), custom_call_target="tpu_custom_call" | custom-call | tf_op jit(solution)/shard_map/pallas_call | solution.py:434
  80.1 1.7 %copy.8 = bf16[512,256]{1,0:T(8,128)(2,1)} copy(bf16[512,256]{1,0:T(8,128)(2,1)} %shard_map.64) | data formatting | bytes 524288

commit v8 on v7

--- a/solution.py
+++ b/solution.py
@@ -27,7 +27,7 @@
 def kernel(
     tok_ref, wq_ref, wk_ref, wv_ref, feat_ref, wo_ref, out_ref,
     tok, w, kv, q, vaug, phik, phiq, feat, fcat, nd, sacc, ssend, srecv, tsend, arecv, nsend, nrecv,
-    excl, tot, ntot, psend, pfx, npre, fsend, frecv, own, attn, rs_send, rs_recv, result,
+    excl, tot, ntot, psend, pfx, npre, fsend, frecv, own, attn, rs_send, rs_recv, result, wout,
     loc_sem, ssem, tok_sem, z_sem, x_sem, sib_sem, a_sem, an_sem, b_sem, bn_sem, c_sem, j_sem, rs_sem,
 ):
     ctx = lax.axis_index("ctx")
@@ -70,8 +70,10 @@
             (feat_ref, feat),
         ])
     ]
-    for copy in loads:
+    for copy in loads[1:]:
         copy.start()
+    for copy in loads[1:]:
+        copy.wait()
     pl.semaphore_wait(barrier, len(greeted))
 
     sends = []
@@ -158,9 +160,9 @@
     for r in range(PIECES):
         for d in range(2):
             tok_send(d, 0, r)
-    for copy in loads:
-        copy.wait()
+    loads[0].start()
     z_send(0)
+    loads[0].wait()
 
     for h in range(2):
         f = feat[h]
@@ -342,6 +344,11 @@
     x_far(2)
     sib_recv(2)
 
+    @pl.loop(0, NY)
+    def _(s):
+        wout[s] = w_rows(s, 3).T
+
+
     for d in range(1, NX):
         xx = turn(x, d, NX)
         recv(ntot.at[xx], bn_sem.at[xx])
@@ -373,9 +380,7 @@
         attn[rows_r, head] = (full[:, :DH] / full[:, DH:]).astype(BF)
 
     def share(dest, r):
-        return lax.dot_general(
-            attn[pl.ds(r * PIECE, PIECE)], w_rows(dest, 3), NT, preferred_element_type=F32
-        )
+        return jnp.dot(attn[pl.ds(r * PIECE, PIECE)], wout[dest], preferred_element_type=F32)
 
     def rs_item(d, step, r, first):
         dest = turn(y, (4 - step) if d == 0 else (step - 4), NY)
@@ -467,6 +472,7 @@
             pltpu.VMEM((2, 4, PIECES, PIECE, WIDTH), BF),
             pltpu.VMEM((2, 4, PIECES, PIECE, WIDTH), BF),
             pltpu.VMEM((TOK, WIDTH), BF),
+            pltpu.VMEM((NY, WIDTH, WIDTH), BF),
             dma((6,)),
             dma((SENDS,)),
             dma((2, 4, PIECES)),

time: 81.9 us -> 81.9 us (level)
  no operation moved by 1% of the time
where the time goes in v8:
time: 81.9 us; the launch traced here: 81.7 us
  Pallas kernels  80 us (98%)
  local copies, waits for them, and re-layouts  1.67 us (2%)
    pallas_call x1, Pallas kernels, body(): pl.pallas_call(kernel, out_shape=jax.ShapeDtypeStruct((TOK, WIDTH), BF),...  80 us
    unnamed x1, local copies, waits for them, and re-layouts  1.67 us

profile of v8, /device:TPU:1, one launch (start us, length us, event | category | flops | bytes accessed | tf_op | source)
XLA Modules:
  0.0 81.7 jit_solution(6228747380871408086)
XLA Ops:
  0.0 80.0 %shard_map.64 = bf16[512,256]{1,0:T(8,128)(2,1)} custom-call(bf16[512,256]{1,0:T(8,128)(2,1)} %tok_ref.1, bf16[32,256]{1,0:T(8,128)(2,1)} %wq_ref.1, bf16[32,256]{1,0:T(8,128)(2,1)} %wk_ref.1, bf16[32,256]{1,0:T(8,128)(2,1)} %wv_ref.1, f32[2,256,128]{2,1,0:T(8,128)} %feat_ref.1, bf16[32,256]{1,0:T(8,128)(2,1)} %bitcast.1), custom_call_target="tpu_custom_call" | custom-call | tf_op jit(solution)/shard_map/pallas_call | solution.py:439
  80.0 1.7 %copy.8 = bf16[512,256]{1,0:T(8,128)(2,1)} copy(bf16[512,256]{1,0:T(8,128)(2,1)} %shard_map.64) | data formatting | bytes 524288
